TPU v7x, 128 devices: a whole 4x4x4 slice. The times are simulated.
128 devices in a mesh: section: 2 (over core), edata: 4 (over y), expert: 16 (over x, z).
Axes of the slice: x: 4, y: 4, z: 4, core: 2. Of those that a mesh axis runs over, the one named last changes fastest.
Arguments:
- hidden_in: bfloat16 [2, 8192, 2048], P('section', ('edata', 'expert')), may hold values from -6 to 6
- out_grad: bfloat16 [2, 8192, 2048], P('section', ('edata', 'expert')), may hold values from -16 to 16
- routes: int32 [2, 8192, 8], P('section', ('edata', 'expert')), may hold values from 0 to 15, all different within a row; in each aligned block of 128 rows (0 to 127, 128 to 255, ..., all dimensions but the last counted through in order) at most 72 rows name the same one
- gates: float32 [2, 8192, 8], P('section', ('edata', 'expert')), may hold values from 0.05 to 0.5
- w_gate_up: bfloat16 [2, 16, 2048, 1536], P('section', 'expert'), may hold values from -0.125 to 0.125
- w_down: bfloat16 [2, 16, 768, 2048], P('section', 'expert'), may hold values from -0.21875 to 0.21875
Outputs:
- upstream_grad: bfloat16 [2, 8192, 2048], P('section', ('edata', 'expert'))
- gate_up_grad: bfloat16 [2, 16, 2048, 1536], P('section', 'expert', 'edata')
- down_grad: bfloat16 [2, 16, 768, 2048], P('section', 'expert', None, 'edata')
Inputs may be any that keep to these rules, and one draw needn't show every extreme that they name: `routes`: the 8 experts of a token are distinct. In the 128 tokens of one device no expert is chosen more than 72 times, a bound that some block reaches.
All inputs are finite; a program needn't handle non-finite values.
Results may differ from a plain program's by a relative error of at most 0.0058.
Values may be sent and summed in bfloat16 or wider, within the bound.
No kernel may reach another device: no remote copies, remote signals or barrier semaphores. Data moves between devices by JAX's collectives and lax.ppermute only.
A program may use at most 192 MiB of HBM per device.

v0:
```python
import functools

import jax
import jax.numpy as jnp
from jax import lax
from jax.experimental import pallas as pl
from jax.experimental.pallas import tpu as pltpu
from jax.sharding import PartitionSpec as P

BF16 = jnp.bfloat16
F32 = jnp.float32
OFF = (0, 1, 3, 2)
SIDE = 4
LANES = 128
MIB = 1024 * 1024


def params(steps):
    return pltpu.CompilerParams(
        vmem_limit_bytes=58 * MIB, dimension_semantics=("arbitrary",) * steps
    )


SCALARS = pl.BlockSpec(memory_space=pltpu.SMEM)
FAR = pl.BlockSpec(memory_space=pl.ANY)


def begun(src, dst, sem):
    copy = pltpu.make_async_copy(src, dst, sem)
    copy.start()
    return copy


def expert_at(me_ref, dx, dz):
    x, z = lax.div(me_ref[0], SIDE), lax.rem(me_ref[0], SIDE)
    return lax.rem(x + dx, SIDE) * SIDE + lax.rem(z + dz, SIDE)


def home_of(me_ref, i, j):
    return expert_at(me_ref, SIDE - OFF[j], SIDE - OFF[i])


def held(shape, index):
    return pl.BlockSpec(shape, index, pipeline_mode=pl.Buffered(1))


def cost(flops, moved):
    return pl.CostEstimate(flops=int(flops), bytes_accessed=int(moved), transcendentals=0)


def moved_along(block, axis, distance):
    if axis == "edata" or axis == "section":
        size = lax.axis_size(axis)
        return lax.ppermute(block, axis, [(i, (i + distance) % size) for i in range(size)])
    pairs = []
    for a in range(SIDE):
        for b in range(SIDE):
            if axis == "x":
                pairs.append((a * SIDE + b, (a + distance) % SIDE * SIDE + b))
            else:
                pairs.append((a * SIDE + b, a * SIDE + (b + distance) % SIDE))
    return lax.ppermute(block, "expert", pairs)


def iota(shape, dim):
    return lax.broadcasted_iota(jnp.int32, shape, dim)


def dot(a, b, da=1, db=0):
    return lax.dot_general(a, b, (((da,), (db,)), ((), ())), preferred_element_type=F32)


def prep_kernel(experts, routes_ref, gates_ref, x_ref, g_ref, xe_ref, ge_ref, tail_ref):
    tok, width = x_ref.shape
    topk = routes_ref.shape[0]
    expert = lax.rem(iota((LANES, tok), 0), experts)
    full = jnp.zeros((LANES, tok), F32)
    for k in range(topk):
        full += jnp.where(routes_ref[k : k + 1, :] == expert, gates_ref[k : k + 1, :], 0.0)
    full = full.T
    lane = iota((tok, LANES), 1)
    high = full.astype(BF16).astype(F32)
    rest = full - high
    middle = rest.astype(BF16).astype(F32)
    low = rest - middle
    piece = jnp.where(lane < 2 * experts, middle, jnp.where(lane < 3 * experts, low, 0.0))
    piece = jnp.where(lane < experts, high, piece).astype(BF16)
    for src, dst in ((x_ref, xe_ref), (g_ref, ge_ref)):
        dst[:, :width] = src[...]
        dst[:, width:] = piece
    tail_ref[...] = piece


def prep(routes, gates, x, g, experts):
    tok, width = x.shape
    shape = jax.ShapeDtypeStruct((tok, width + LANES), BF16)
    return pl.pallas_call(
        functools.partial(prep_kernel, experts),
        out_shape=(shape, shape, jax.ShapeDtypeStruct((tok, LANES), BF16)),
        compiler_params=params(0),
        name="prep",
    )(routes, gates, x, g)


def places(piece, experts, blocks):
    rows = piece.shape[0]
    tok = rows // blocks
    r, c = iota((rows, rows), 0), iota((rows, rows), 1)
    upto = jnp.where((c <= r) & (lax.div(c, tok) == lax.div(r, tok)), 1.0, 0.0).astype(BF16)
    lane = iota((rows, LANES), 1)
    mask = jnp.where((lane < experts) & (piece.astype(F32) > 0.0), 1.0, 0.0)
    return (dot(upto, mask.astype(BF16)) * mask).astype(BF16)


def pack_kernel(scale, experts, cap, steps_to, me_ref, *refs):
    blocks, outs = refs[:4], refs[4:-5]
    rows_v, packed_v, table_v, in_sems, out_sems = refs[-5:]
    count = len(outs)
    eids = [expert_at(me_ref, dx, dz) for dx, dz in steps_to]
    pair = 2 * cap
    tok, width = blocks[0].shape[0], outs[0].shape[1]
    steps, step = packed_v.shape[0], packed_v.shape[3]
    pieces = [slice(width, width + LANES)] + [slice(t * step, (t + 1) * step) for t in range(steps)]
    loads = []
    for n, cols in enumerate(pieces):
        for b in range(4):
            part = rows_v.at[b // 2, pl.ds(b % 2 * tok, tok), cols]
            loads.append(begun(blocks[b].at[:, cols], part, in_sems.at[n, b]))
    for load in loads[:4]:
        load.wait()
    lane = iota((pair, LANES), 1)
    second = jnp.where(iota((pair, 2 * tok), 1) >= tok, cap, 0)
    place = iota((pair, 2 * tok), 0) + 1 - second
    place = jnp.where(place > 0, place, -1).astype(F32)
    factors = []
    for p in range(2):
        piece = rows_v[p, :, width:]
        known = places(piece, experts, 2)
        for j in range(count):
            choose = jnp.where(lane == eids[j], 1.0, 0.0).astype(BF16)
            found = dot(choose, known, 1, 1)
            table = jnp.where(found == place, 1.0, 0.0).astype(BF16)
            table_v[p, j * pair : (j + 1) * pair, :] = table
            if scale:
                mine = (lax.rem(lane, experts) == eids[j]) & (lane < 3 * experts)
                gate = jnp.where(mine, dot(table, piece), 0.0)
                factors.append(jnp.sum(gate, axis=1, keepdims=True))
    stores = []
    for t in range(steps):
        for load in loads[4 * t + 4 : 4 * t + 8]:
            load.wait()
        for p in range(2):
            packed = dot(table_v[p], rows_v[p, :, pieces[t + 1]])
            for j in range(count):
                part = packed[j * pair : (j + 1) * pair]
                if scale:
                    part = part * factors[p * count + j]
                packed_v[t, j, p * pair : (p + 1) * pair, :] = part.astype(BF16)
        for j in range(count):
            target = outs[j].at[:, pieces[t + 1]]
            stores.append(begun(packed_v.at[t, j], target, out_sems.at[t, j]))
    for store in stores:
        store.wait()


def pack(me, blocks, width, experts, cap, steps_to, scale, name):
    count = len(steps_to)
    tok = blocks[0].shape[0]
    step = 512
    steps = width // step
    pair = 2 * cap
    out = jax.ShapeDtypeStruct((2 * pair, width), BF16)
    return pl.pallas_call(
        functools.partial(pack_kernel, scale, experts, cap, steps_to),
        in_specs=[SCALARS] + [FAR] * 4,
        out_specs=[FAR] * count,
        out_shape=[out] * count,
        scratch_shapes=[
            pltpu.VMEM((2, 2 * tok, width + LANES), BF16),
            pltpu.VMEM((steps, count, 2 * pair, step), BF16),
            pltpu.VMEM((2, count * pair, 2 * tok), BF16),
            pltpu.SemaphoreType.DMA((steps + 1, 4)),
            pltpu.SemaphoreType.DMA((steps, count)),
        ],
        compiler_params=params(0),
        cost_estimate=cost(3e9, 10e6),
        name=name,
    )(me, *blocks)


def home_kernel(experts, cap, tail_ref, rows_ref, grad_ref, out_ref, table_ref):
    tok = tail_ref.shape[0]
    total = experts * cap

    @pl.when(pl.program_id(0) == 0)
    def _():
        choose = jnp.where(iota((LANES, total), 0) == lax.div(iota((LANES, total), 1), cap), 1.0, 0.0)
        found = dot(places(tail_ref[...], experts, 1), choose.astype(BF16))
        place = lax.rem(iota((tok, total), 1), cap) + 1
        table_ref[...] = jnp.where(found == place.astype(F32), 1.0, 0.0).astype(BF16)

    total_grad = dot(table_ref[...], rows_ref[...]) + grad_ref[...].astype(F32)
    out_ref[...] = total_grad.astype(BF16)


def home(tail, rows, grad, experts, cap):
    tok, width = grad.shape
    step = 512
    total = experts * cap
    return pl.pallas_call(
        functools.partial(home_kernel, experts, cap),
        grid=(width // step,),
        in_specs=[
            held((tok, LANES), lambda i: (0, 0)),
            pl.BlockSpec((total, step), lambda i: (0, i)),
            pl.BlockSpec((tok, step), lambda i: (0, i)),
        ],
        out_specs=pl.BlockSpec((tok, step), lambda i: (0, i)),
        out_shape=jax.ShapeDtypeStruct((tok, width), BF16),
        scratch_shapes=[pltpu.VMEM((tok, total), BF16)],
        compiler_params=params(1),
        cost_estimate=cost(3e9, 10e6),
        name="home",
    )(tail, rows, grad)


def up_kernel(count, *refs):
    xs, (wa, wb), outs = refs[:count], refs[count : count + 2], refs[count + 2 :]
    for i in range(count):
        rows = xs[i][...]
        a = dot(rows, wa[...])
        b = dot(rows, wb[...])
        sig = jax.nn.sigmoid(a)
        outs[3 * i][...] = a * sig * b
        outs[3 * i + 1][...] = (b * sig * (1.0 + a * (1.0 - sig))).astype(BF16)
        outs[3 * i + 2][...] = (a * sig).astype(BF16)


def up(xs, wgu):
    count = len(xs)
    rows, width = xs[0].shape
    hidden = wgu.shape[1] // 2
    step = 256
    steps = hidden // step
    kinds = (F32, BF16, BF16) * count
    flat = pl.pallas_call(
        functools.partial(up_kernel, count),
        grid=(steps,),
        in_specs=[held((rows, width), lambda i: (0, 0))] * count
        + [
            pl.BlockSpec((width, step), lambda i: (0, i)),
            pl.BlockSpec((width, step), lambda i: (0, i + steps)),
        ],
        out_specs=[pl.BlockSpec((rows, step), lambda i: (0, i))] * (3 * count),
        out_shape=[jax.ShapeDtypeStruct((rows, hidden), kind) for kind in kinds],
        compiler_params=params(1),
        cost_estimate=cost(3e9, 10e6),
        name="up",
    )(*xs, wgu, wgu)
    return [flat[3 * i : 3 * i + 3] for i in range(count)]


def dh_kernel(count, *refs):
    ss, wd, outs = refs[:count], refs[count], refs[count + 1 :]
    for i in range(count):
        outs[i][...] = dot(ss[i][...], wd[...], 1, 1)


def dh_of(ss, wdown):
    count = len(ss)
    rows, width = ss[0].shape
    hidden = wdown.shape[0]
    step = 256
    return pl.pallas_call(
        functools.partial(dh_kernel, count),
        grid=(hidden // step,),
        in_specs=[held((rows, width), lambda i: (0, 0))] * count
        + [pl.BlockSpec((step, width), lambda i: (i, 0))],
        out_specs=[pl.BlockSpec((rows, step), lambda i: (0, i))] * count,
        out_shape=[jax.ShapeDtypeStruct((rows, hidden), F32)] * count,
        compiler_params=params(1),
        cost_estimate=cost(3e9, 10e6),
        name="dh",
    )(*ss, wdown)


def crossed(parts, j, cap):
    return jnp.concatenate([part[j * cap : (j + 1) * cap, :] for part in parts], axis=0)


def activations(rows, w, t, hidden):
    a = dot(rows, w[:, tile(t, 256)])
    b = dot(rows, w[:, tile(t + hidden // 256, 256)])
    sig = jax.nn.sigmoid(a)
    return a * sig * b, (b * sig * (1.0 + a * (1.0 - sig)), a * sig)


def tile(t, step):
    return pl.ds(pl.multiple_of(t * step, step), step)


def gate_up_load(w, w_v, sems, hidden, t, k):
    part = tile(t + k * (hidden // 256), 256)
    return pltpu.make_async_copy(w.at[:, part], w_v.at[:, part], sems.at[t, k])


def gate_up_loads(w, w_v, sems, hidden):
    for t in range(hidden // 256):
        for k in range(2):
            gate_up_load(w, w_v, sems, hidden, t, k).start()


def row_load(w, w_v, sems, t, step):
    return pltpu.make_async_copy(w.at[tile(t, step), :], w_v.at[tile(t, step), :], sems.at[t])


def send_rows(d_v, w_v, blocks, cap, me_ref, rows_v, out, sems, ready=None):
    hidden = w_v.shape[1] // 2

    def copy_of(t, n, i, j):
        target = out.at[home_of(me_ref, i, j), :, tile(t, 512)]
        return pltpu.make_async_copy(rows_v.at[t, n], target, sems.at[t, n])

    @pl.loop(0, w_v.shape[0] // 512)
    def _(t):
        if ready is not None:
            ready(t)
        w = w_v[tile(t, 512), :]
        part = dot(d_v[0], w[:, :hidden], 1, 1) + dot(d_v[1], w[:, hidden:], 1, 1)
        for n, (i, j) in enumerate(blocks):
            rows_v[t, n] = part[n * cap : (n + 1) * cap].astype(BF16)
            copy_of(t, n, i, j).start()

    @pl.loop(0, w_v.shape[0] // 512)
    def _(t):
        for n, (i, j) in enumerate(blocks):
            copy_of(t, n, i, j).wait()


def middle_kernel(cap, me_ref, *refs):
    w, wd, xs, ss, fs, dh0 = refs[0], refs[1], refs[2:4], refs[4:6], refs[6:8], refs[8]
    h_out, tail_out, dh_out, out, ds = refs[9:11], refs[11], refs[12], refs[13], refs[14:16]
    w_v, wd_v, x_v, s_v, h_v, f_v, dh_v, tail_v, dh_tail_v, d_v, e_v, rows_v = refs[16:28]
    w_sems, wd_sems, in_sems, out_sems, row_sems = refs[28:]
    rows = xs[0].shape[0]
    hidden = wd.shape[0]
    edge = 3 * cap - 8
    x_loads = [begun(xs[n], x_v.at[n], in_sems.at[n]) for n in range(2)]
    gate_up_loads(w, w_v, w_sems, hidden)
    s_loads = [begun(ss[n], s_v.at[n], in_sems.at[2 + n]) for n in range(2)]
    for t in range(hidden // 256):
        row_load(wd, wd_v, wd_sems, t, 256).start()
    f_loads = [begun(fs[k], f_v.at[k, 0], in_sems.at[4 + k]) for k in range(2)]
    f_loads.append(begun(dh0, dh_v.at[0], in_sems.at[6]))
    for load in x_loads:
        load.wait()
    @pl.loop(0, hidden // 256)
    def _(t):
        for k in range(2):
            gate_up_load(w, w_v, w_sems, hidden, t, k).wait()
        for n in range(2):
            h, factors = activations(x_v[n], w_v, t, hidden)
            h_v[n, :, tile(t, 256)] = h
            for k in range(2):
                f_v[k, n + 1, :, tile(t, 256)] = factors[k].astype(BF16)

    copies = [begun(h_v.at[n], h_out[n], out_sems.at[n]) for n in range(2)]
    for load in s_loads:
        load.wait()
    @pl.loop(0, hidden // 256)
    def _(t):
        row_load(wd, wd_v, wd_sems, t, 256).wait()
        for n in range(2):
            dh_v[n + 1, :, tile(t, 256)] = dot(s_v[n], wd_v[tile(t, 256), :], 1, 1)

    for load in f_loads:
        load.wait()
    for j in range(3):
        dh_tail_v[j * cap : (j + 1) * cap, :] = dh_v[j, 3 * cap :, :]
        for k in range(2):
            tail_v[k, j] = f_v[k, j, edge:, :]
    copies.append(begun(dh_tail_v, dh_out, out_sems.at[2]))
    copies.append(begun(tail_v, tail_out, out_sems.at[3]))
    for k in range(2):
        @pl.loop(0, hidden // 256)
        def _(t):
            cols = tile(t, 256)
            chunks = [dh_v[j, :, cols] for j in range(3)]
            kept = []
            for i in range(3):
                factor = f_v[k, i, :, cols].astype(F32)[: 3 * cap]
                product = crossed(chunks, i, cap) * factor
                kept.append(product)
                whole = jnp.concatenate([product, jnp.zeros((cap, 256), F32)], axis=0)
                d_v[k, i * rows : (i + 1) * rows, cols] = whole.astype(BF16)
            e_v[k, :, cols] = jnp.concatenate(kept, axis=0).astype(BF16)

        copies.append(begun(d_v.at[k], ds[k].at[pl.ds(0, 3 * rows), :], out_sems.at[4 + k]))
    blocks = [(i, j) for i in range(3) for j in range(3)]
    send_rows(e_v, w_v, blocks, cap, me_ref, rows_v, out, row_sems)
    for copy in copies:
        copy.wait()


def middle(me, wgu, wdown, xs, ss, factors, dh0, cap):
    rows, width = xs[0].shape
    hidden = wdown.shape[0]
    steps = width // 512
    h = jax.ShapeDtypeStruct((rows, hidden), F32)
    tail = jax.ShapeDtypeStruct((2, 3, cap + 8, hidden), BF16)
    dab = jax.ShapeDtypeStruct((SIDE * rows, hidden), BF16)
    slots = jax.ShapeDtypeStruct((SIDE * SIDE, cap, width), BF16)
    h1, h2, tails, dh_tail, slots, da, db = pl.pallas_call(
        functools.partial(middle_kernel, cap),
        in_specs=[SCALARS] + [FAR] * 9,
        out_specs=[FAR] * 7,
        out_shape=[h, h, tail, jax.ShapeDtypeStruct((3 * cap, hidden), F32), slots, dab, dab],
        scratch_shapes=[
            pltpu.VMEM((width, 2 * hidden), BF16),
            pltpu.VMEM((hidden, width), BF16),
            pltpu.VMEM((2, rows, width), BF16),
            pltpu.VMEM((2, rows, width), BF16),
            pltpu.VMEM((2, rows, hidden), F32),
            pltpu.VMEM((2, 3, rows, hidden), BF16),
            pltpu.VMEM((3, rows, hidden), F32),
            pltpu.VMEM((2, 3, cap + 8, hidden), BF16),
            pltpu.VMEM((3 * cap, hidden), F32),
            pltpu.VMEM((2, 3 * rows, hidden), BF16),
            pltpu.VMEM((2, 9 * cap, hidden), BF16),
            pltpu.VMEM((steps, 9, cap, 512), BF16),
            pltpu.SemaphoreType.DMA((hidden // 256, 2)),
            pltpu.SemaphoreType.DMA((hidden // 256,)),
            pltpu.SemaphoreType.DMA((7,)),
            pltpu.SemaphoreType.DMA((6,)),
            pltpu.SemaphoreType.DMA((steps, 9)),
        ],
        compiler_params=params(0),
        cost_estimate=cost(3e9, 10e6),
        name="middle",
    )(me, wgu, wdown, *xs, *ss, *factors, dh0)
    return [h1, h2], tails, dh_tail, slots, [da, db]


def last_x_kernel(cap, me_ref, *refs):
    w, x, hs, dh_tail = refs[0], refs[1], refs[2:5], refs[5]
    turned_out, tail_out, out, ds = refs[9], refs[10], refs[11], refs[12:14]
    w_v, x_v, h_v, f_v, dh_v, turned_v, d_v, e_v, rows_v = refs[14:23]
    w_sems, in_sems, out_sems, row_sems = refs[23:]
    rows = x.shape[0]
    hidden = w.shape[1] // 2
    edge = 3 * cap - 8
    x_load = begun(x, x_v, in_sems.at[0])
    gate_up_loads(w, w_v, w_sems, hidden)
    loads = [begun(hs[n], h_v.at[n], in_sems.at[1 + n]) for n in range(3)]
    loads.append(begun(dh_tail, dh_v, in_sems.at[4]))
    x_load.wait()
    @pl.loop(0, hidden // 256)
    def _(t):
        for k in range(2):
            gate_up_load(w, w_v, w_sems, hidden, t, k).wait()
        h, factors = activations(x_v[...], w_v, t, hidden)
        h_v[3, :, tile(t, 256)] = h
        for k in range(2):
            f_v[k, :, tile(t, 256)] = factors[k].astype(BF16)

    for load in loads:
        load.wait()
    copies = [begun(f_v.at[:, pl.ds(edge, cap + 8), :], tail_out, out_sems.at[0])]
    @pl.loop(0, hidden // 256)
    def _(t):
        cols = tile(t, 256)
        parts = [h_v[n, :, cols] for n in range(SIDE)]
        whole = jnp.concatenate([crossed(parts, j, cap) for j in range(SIDE)], axis=0)
        turned_v[cols, :] = whole.T.astype(BF16)
        for k in range(2):
            product = dh_v[:, cols] * f_v[k, :, cols].astype(F32)[: 3 * cap]
            e_v[k, :, cols] = product.astype(BF16)
            whole = jnp.concatenate([product, jnp.zeros((cap, 256), F32)], axis=0)
            d_v[k, :, cols] = whole.astype(BF16)

    copies.append(begun(turned_v, turned_out, out_sems.at[1]))
    for k in range(2):
        copies.append(begun(d_v.at[k], ds[k].at[pl.ds(3 * rows, rows), :], out_sems.at[2 + k]))
    blocks = [(3, j) for j in range(3)]
    send_rows(e_v, w_v, blocks, cap, me_ref, rows_v, out, row_sems)
    for copy in copies:
        copy.wait()


def last_x(me, wgu, x, hs, dh_tail, slots, ds, cap):
    rows, width = x.shape
    hidden = wgu.shape[1] // 2
    steps = width // 512
    turned_h, tail, slots, da, db = pl.pallas_call(
        functools.partial(last_x_kernel, cap),
        in_specs=[SCALARS] + [FAR] * 9,
        out_specs=[FAR] * 5,
        out_shape=[
            jax.ShapeDtypeStruct((hidden, SIDE * rows), BF16),
            jax.ShapeDtypeStruct((2, cap + 8, hidden), BF16),
        ]
        + [jax.ShapeDtypeStruct(a.shape, BF16) for a in (slots, *ds)],
        input_output_aliases={7: 2, 8: 3, 9: 4},
        scratch_shapes=[
            pltpu.VMEM((width, 2 * hidden), BF16),
            pltpu.VMEM((rows, width), BF16),
            pltpu.VMEM((SIDE, rows, hidden), F32),
            pltpu.VMEM((2, rows, hidden), BF16),
            pltpu.VMEM((3 * cap, hidden), F32),
            pltpu.VMEM((hidden, SIDE * rows), BF16),
            pltpu.VMEM((2, rows, hidden), BF16),
            pltpu.VMEM((2, 3 * cap, hidden), BF16),
            pltpu.VMEM((steps, 3, cap, 512), BF16),
            pltpu.SemaphoreType.DMA((hidden // 256, 2)),
            pltpu.SemaphoreType.DMA((5,)),
            pltpu.SemaphoreType.DMA((4,)),
            pltpu.SemaphoreType.DMA((steps, 3)),
        ],
        compiler_params=params(0),
        cost_estimate=cost(3e9, 10e6),
        name="last_x",
    )(me, wgu, x, *hs, dh_tail, slots, *ds)
    return turned_h, tail, slots, [da, db]


AHEAD = (2, 1, 3)
SPOTS = (((0, 0), (1, 1)), ((2, 0), (0, 1)), ((1, 0), (2, 1)))


def put_halves(k, part, sent_v, wait_v, outs, sems):
    half = part.shape[0] // 2
    copies = []
    for side in range(2):
        out, row = SPOTS[k][side]
        piece = part[side * half : (side + 1) * half]
        if out == 2:
            staged = wait_v.at[row]
            staged[...] = piece
        else:
            staged = sent_v.at[out, row]
            staged[...] = piece.astype(BF16)
        target = outs[out].at[row * half : (row + 1) * half, :]
        copies.append(begun(staged, target, sems.at[k, side]))
    return copies


def ahead_of(place_ref, ahead, size):
    start = lax.rem(place_ref[0] + ahead, SIDE) * size
    return pl.ds(pl.multiple_of(start, size), size)


def message_outs(rows, cols):
    return [jax.ShapeDtypeStruct((rows, cols), kind) for kind in (BF16, BF16, F32)]


def message_scratch(rows, cols):
    return [
        pltpu.VMEM((2, 2, rows // 2, cols), BF16),
        pltpu.VMEM((2, rows // 2, cols), F32),
        pltpu.SemaphoreType.DMA((3, 2)),
    ]


def last_s_kernel(cap, me_ref, place_ref, *refs):
    turned, ss, wd, tails, tail, w = refs[0], refs[1:5], refs[5], refs[6], refs[7], refs[8]
    outs, out, ds = refs[10:13], refs[13], refs[14:16]
    turned_v, q_v, s_v, wd_v, f_v, d_v, w_v, rows_v = refs[16:24]
    sent_v, wait_v, message_sems, in_sems, q_sems, wd_sems, w_sems, out_sems, row_sems = refs[24:]
    rows, width = ss[0].shape
    hidden = wd.shape[0]
    turned_load = begun(turned, turned_v, in_sems.at[0])
    q_loads = []
    for k, ahead in enumerate(AHEAD):
        cols = ahead_of(place_ref, ahead, width // SIDE)
        for j in range(SIDE):
            part = q_v.at[k, pl.ds(j * rows, rows), :]
            q_loads.append(begun(ss[j].at[:, cols], part, q_sems.at[k, j]))
    s_load = begun(ss[3], s_v, in_sems.at[1])
    for t in range(hidden // 256):
        row_load(wd, wd_v, wd_sems, t, 256).start()
    loads = [begun(tails, f_v.at[:, pl.ds(0, 3)], in_sems.at[2])]
    loads.append(begun(tail, f_v.at[:, 3], in_sems.at[3]))
    for t in range(w.shape[0] // 512):
        row_load(w, w_v, w_sems, t, 512).start()
    turned_load.wait()
    copies = []
    for k in range(3):
        for load in q_loads[4 * k : 4 * k + 4]:
            load.wait()
        part = dot(turned_v[...], q_v[k])
        copies += put_halves(k, part, sent_v, wait_v, outs, message_sems)
    s_load.wait()
    for load in loads:
        load.wait()
    @pl.loop(0, hidden // 256)
    def _(t):
        row_load(wd, wd_v, wd_sems, t, 256).wait()
        cols = tile(t, 256)
        dh = dot(s_v[...], wd_v[cols, :], 1, 1)
        for k in range(2):
            factors = [f_v[k, i, :, cols].astype(F32)[8:] for i in range(SIDE)]
            d_v[k, :, cols] = (dh * jnp.concatenate(factors, axis=0)).astype(BF16)

    copies += [begun(d_v.at[k], ds[k], out_sems.at[k]) for k in range(2)]
    blocks = [(i, 3) for i in range(SIDE)]
    ready = lambda t: row_load(w, w_v, w_sems, t, 512).wait()
    send_rows(d_v, w_v, blocks, cap, me_ref, rows_v, out, row_sems, ready)
    for copy in copies:
        copy.wait()


def last_s(me, place, turned_h, ss, wdown, tails, tail, wgu, slots, cap):
    rows, width = ss[0].shape
    hidden, total = turned_h.shape
    quarter = width // SIDE
    steps = width // 512
    dab = jax.ShapeDtypeStruct((rows, hidden), BF16)
    *down, slots, da, db = pl.pallas_call(
        functools.partial(last_s_kernel, cap),
        in_specs=[SCALARS] * 2 + [FAR] * 10,
        out_specs=[FAR] * 6,
        out_shape=message_outs(hidden, quarter)
        + [jax.ShapeDtypeStruct(slots.shape, BF16), dab, dab],
        input_output_aliases={11: 3},
        scratch_shapes=[
            pltpu.VMEM((hidden, total), BF16),
            pltpu.VMEM((3, total, quarter), BF16),
            pltpu.VMEM((rows, width), BF16),
            pltpu.VMEM((hidden, width), BF16),
            pltpu.VMEM((2, SIDE, cap + 8, hidden), BF16),
            pltpu.VMEM((2, rows, hidden), BF16),
            pltpu.VMEM((width, 2 * hidden), BF16),
            pltpu.VMEM((steps, SIDE, cap, 512), BF16),
        ]
        + message_scratch(hidden, quarter)
        + [
            pltpu.SemaphoreType.DMA((4,)),
            pltpu.SemaphoreType.DMA((3, SIDE)),
            pltpu.SemaphoreType.DMA((hidden // 256,)),
            pltpu.SemaphoreType.DMA((steps,)),
            pltpu.SemaphoreType.DMA((2,)),
            pltpu.SemaphoreType.DMA((steps, SIDE)),
        ],
        compiler_params=params(0),
        cost_estimate=cost(1, 1),
        name="last_s",
    )(me, place, turned_h, *ss, wdown, tails, tail, wgu, slots)
    return down, slots, [da, db]


def down_own_kernel(place_ref, *refs):
    turned_ref, ss, out = refs[0], refs[1:5], refs[5]
    out[...] = dot(turned_ref[...], jnp.concatenate([s[...] for s in ss], axis=0))


def down_own(place, turned_h, ss):
    hidden, total = turned_h.shape
    rows, width = ss[0].shape
    quarter = width // SIDE
    return pl.pallas_call(
        down_own_kernel,
        grid_spec=pltpu.PrefetchScalarGridSpec(
            num_scalar_prefetch=1,
            grid=(2,),
            in_specs=[pl.BlockSpec((hidden // 2, total), lambda i, place: (i, 0))]
            + [held((rows, quarter), lambda i, place: (0, place[0]))] * 4,
            out_specs=pl.BlockSpec((hidden // 2, quarter), lambda i, place: (i, 0)),
        ),
        out_shape=jax.ShapeDtypeStruct((hidden, quarter), F32),
        compiler_params=params(1),
        cost_estimate=cost(1, 1),
        name="down_own",
    )(place, turned_h, *ss)


def gate_up_kernel(cap, place_ref, *refs):
    early, late, xs, outs, ds = refs[:2], refs[2:4], refs[4:8], refs[8:11], refs[11:13]
    d_v, late_v, x_v, sent_v, wait_v, out_sems, d_sems, x_sems = refs[13:]
    rows, width = xs[0].shape
    size = width // SIDE
    loads = []
    for k in range(2):
        loads.append(begun(early[k], d_v.at[k], d_sems.at[0, k]))
        loads.append(begun(late[k], late_v.at[k], d_sems.at[1, k]))
    for k, ahead in enumerate(AHEAD):
        cols = ahead_of(place_ref, ahead, size)
        for i in range(SIDE):
            part = x_v.at[k, pl.ds(i * rows, rows), :]
            loads.append(begun(xs[i].at[:, cols], part, x_sems.at[k, i]))
    for load in loads[:4]:
        load.wait()
    edge = 3 * cap - 8
    copies = []
    for k in range(2):
        fresh = late_v[k].astype(F32)
        for i in range(SIDE):
            at = slice(i * rows + edge, (i + 1) * rows)
            old = d_v[k, at, :].astype(F32)[:8]
            new = fresh[i * cap : (i + 1) * cap]
            d_v[k, at, :] = jnp.concatenate([old, new], axis=0).astype(BF16)
        copies.append(begun(d_v.at[k], ds[k], d_sems.at[2, k]))
    for k in range(3):
        for load in loads[4 * k + 4 : 4 * k + 8]:
            load.wait()
        turned_x = x_v[k].T
        part = jnp.concatenate([dot(turned_x, d_v[0]), dot(turned_x, d_v[1])], axis=1)
        copies += put_halves(k, part, sent_v, wait_v, outs, out_sems)
    for copy in copies:
        copy.wait()


def gate_up_parts(place, early, late, xs, cap):
    rows, width = xs[0].shape
    total, hidden = early[0].shape
    quarter = width // SIDE
    out = jax.ShapeDtypeStruct((total, hidden), BF16)
    *messages, da, db = pl.pallas_call(
        functools.partial(gate_up_kernel, cap),
        in_specs=[SCALARS] + [FAR] * 8,
        out_specs=[FAR] * 5,
        out_shape=message_outs(quarter, 2 * hidden) + [out, out],
        scratch_shapes=[
            pltpu.VMEM((2, total, hidden), BF16),
            pltpu.VMEM((2, *late[0].shape), BF16),
            pltpu.VMEM((3, total, quarter), BF16),
        ]
        + message_scratch(quarter, 2 * hidden)
        + [pltpu.SemaphoreType.DMA((3, 2)), pltpu.SemaphoreType.DMA((3, SIDE))],
        compiler_params=params(0),
        cost_estimate=cost(1, 1),
        name="gate_up_parts",
    )(place, *early, *late, *xs)
    return messages, [da, db]


def gate_up_own_kernel(place_ref, *refs):
    xs, ds, out = refs[:4], refs[4:6], refs[6]
    rows = jnp.concatenate([x[...] for x in xs], axis=0).T
    out[...] = jnp.concatenate([dot(rows, d[...]) for d in ds], axis=1)


def gate_up_own(place, xs, ds):
    rows, width = xs[0].shape
    total, hidden = ds[0].shape
    half = width // SIDE // 2
    return pl.pallas_call(
        gate_up_own_kernel,
        grid_spec=pltpu.PrefetchScalarGridSpec(
            num_scalar_prefetch=1,
            grid=(2,),
            in_specs=[pl.BlockSpec((rows, half), lambda i, place: (0, 2 * place[0] + i))] * 4
            + [held((total, hidden), lambda i, place: (0, 0))] * 2,
            out_specs=pl.BlockSpec((half, 2 * hidden), lambda i, place: (i, 0)),
        ),
        out_shape=jax.ShapeDtypeStruct((2 * half, 2 * hidden), F32),
        compiler_params=params(1),
        cost_estimate=cost(200e9, 10e6),
        name="gate_up_own",
    )(place, *xs, *ds)


def around(first, axis):
    return [first] + [moved_along(first, axis, OFF[b]) for b in range(1, SIDE)]


def spread(outs, axis, work):
    near = [moved_along(outs[j], axis, OFF[j]) for j in (1, 2)]
    done = work(outs[0])
    far, near[0], near[1], *done = lax.optimization_barrier((outs[3], *near, *done))
    return [outs[0], *near, moved_along(far, axis, OFF[3])], done


def ring_first(first_up, first_down, wait):
    return moved_along(first_up, "edata", 1), moved_along(first_down, "edata", -1)


def ring_second(up1, down1, first_up, first_down, wait):
    half = wait.shape[0] // 2
    second_up = (wait[:half] + up1[:half].astype(F32)).astype(BF16)
    second_down = (wait[half:] + down1[half:].astype(F32)).astype(BF16)
    return moved_along(second_up, "edata", 1), moved_along(second_down, "edata", -1)


def ring_own(own, up1, down1):
    half = own.shape[0] // 2
    return own + jnp.concatenate([down1[:half], up1[half:]], axis=0).astype(F32)


def ring_last(total, up2, down2):
    return (total + jnp.concatenate([up2, down2], axis=0).astype(F32)).astype(BF16)


def body(hidden_in, out_grad, routes, gates, w_gate_up, w_down):
    tok = hidden_in.shape[1]
    width = hidden_in.shape[2]
    topk = routes.shape[2]
    experts = lax.axis_size("expert")
    cap = min(tok, tok * topk * 9 // (8 * experts))
    wgu, wdown = w_gate_up[0, 0], w_down[0, 0]
    me = lax.axis_index("expert").astype(jnp.int32).reshape(1)
    place = lax.axis_index("edata").astype(jnp.int32).reshape(1)

    xe, ge, tail = prep(routes[0].T, gates[0].T, hidden_in[0], out_grad[0], experts)
    xblocks = around(xe, "x")
    gblocks = around(ge, "z")
    def packed(blocks, scale, name, which):
        steps_to = tuple((OFF[j], 0) if scale else (0, OFF[j]) for j in which)
        return list(pack(me, blocks, width, experts, cap, steps_to, scale, name))

    xnear = packed(xblocks, False, "pack_rows", (1, 2))
    xnear[0], gblocks[0] = lax.optimization_barrier((xnear[0], gblocks[0]))
    gnear = packed(gblocks, True, "pack_scaled", (1, 2))
    xblocks[0], gnear[0] = lax.optimization_barrier((xblocks[0], gnear[0]))
    x0, xfar = packed(xblocks, False, "pack_rows_rest", (0, 3))
    s0, sfar = packed(gblocks, True, "pack_scaled_rest", (0, 3))
    xs, (h0, *factors) = spread([x0, *xnear, xfar], "z", lambda rows: up([rows], wgu)[0])
    ss, (dh0,) = spread([s0, *gnear, sfar], "x", lambda rows: dh_of([rows], wdown))
    hs, tails, dh_tail, slots, early = middle(
        me, wgu, wdown, xs[1:3], ss[1:3], factors, dh0, cap
    )
    turned_h, last_tail, slots, early = last_x(
        me, wgu, xs[3], [h0, *hs], dh_tail, slots, early, cap
    )
    last, slots, turned_h = lax.optimization_barrier((ss[3], slots, turned_h))
    ss = ss[:3] + [last]
    down, rows, late = last_s(me, place, turned_h, ss, wdown, tails, last_tail, wgu, slots, cap)
    down_first = ring_first(*down)
    returned = lax.all_to_all(rows, "expert", split_axis=0, concat_axis=0, tiled=True)
    rows, *late = lax.optimization_barrier((rows, *late))
    gate_up, ds = gate_up_parts(place, early, late, xs, cap)
    gate_up[0], gate_up[1], *down_first = lax.optimization_barrier((gate_up[0], gate_up[1], *down_first))
    gate_up_first = ring_first(*gate_up)
    wait, da, db, turned_h = lax.optimization_barrier((gate_up[2], *ds, turned_h))
    gate_up = [*gate_up[:2], wait]
    own_down = down_own(place, turned_h, ss)
    own_gate_up = gate_up_own(place, xs, [da, db])
    own_down, own_gate_up, *gate_up_first = lax.optimization_barrier(
        (own_down, own_gate_up, *gate_up_first)
    )
    down_second = ring_second(*down_first, *down)
    gate_up_second = ring_second(*gate_up_first, *gate_up)
    down_grad = ring_last(ring_own(own_down, *down_first), *down_second)
    gate_up_grad = ring_last(ring_own(own_gate_up, *gate_up_first), *gate_up_second)

    layer = home(tail, returned.reshape(experts * cap, width), out_grad[0], experts, cap)
    upstream = moved_along(layer, "section", -1)
    return (upstream[None], gate_up_grad[None, None], down_grad[None, None])


def solution(mesh):
    return jax.shard_map(
        body,
        mesh=mesh,
        in_specs=(
            P("section", ("edata", "expert"), None),
            P("section", ("edata", "expert"), None),
            P("section", ("edata", "expert"), None),
            P("section", ("edata", "expert"), None),
            P("section", "expert", None, None),
            P("section", "expert", None, None),
        ),
        out_specs=(
            P("section", ("edata", "expert"), None),
            P("section", "expert", "edata", None),
            P("section", "expert", None, "edata"),
        ),
        check_vma=False,
    )
```

profile of v0, /device:TPU:0, one launch (start us, length us, event | category | flops | bytes accessed | tf_op | source)
XLA Modules:
  0.0 203.6 jit_solution(7691999017333378052)
XLA Ops:
  0.6 2.4 %prep.1 = (bf16[128,2176]{1,0:T(8,128)(2,1)}, bf16[128,2176]{1,0:T(8,128)(2,1)}, bf16[128,128]{1,0:T(8,128)(2,1)}) custom-call(s32[8,128]{1,0:T(8,128)} %bitcast.30, f32[8,128]{1,0:T(8,128)} %bitcast.31, bf16[128,2048]{1,0:T(8,128)(2,1)} %bitcast.26, bf16[128,2048]{1,0:T(8,128)(2,1)} %bitcast.27), custom_call_target="tpu_custom_call" | custom-call | tf_op jit(solution)/shard_map/prep/pallas_call | solution.py:97
  3.0 3.1 %collective-permute-start.2 = (bf16[128,2176]{1,0:T(8,128)(2,1)}, bf16[128,2176]{1,0:T(8,128)(2,1)S(1)}, u32[]{:S(2)}, u32[]{:S(2)}) collective-permute-start(bf16[128,2176]{1,0:T(8,128)(2,1)} %get-tuple-element.82.refs_0_), channel_id=1, source_target_pairs={{0,8},{1,9},{2,10},{3,11},{4,12},{5,13},{6,14},{7,15},{8,0},{9,1},... | collective-permute-start | bytes 1671176 | tf_op jit(solution)/shard_map/ppermute | solution.py:62
  8.1 3.9 %collective-permute-start.5 = (bf16[128,2176]{1,0:T(8,128)(2,1)}, bf16[128,2176]{1,0:T(8,128)(2,1)S(1)}, u32[]{:S(2)}, u32[]{:S(2)}) collective-permute-start(bf16[128,2176]{1,0:T(8,128)(2,1)} %get-tuple-element.75.refs_0_), channel_id=1, source_target_pairs={{0,2},{1,3},{2,0},{3,1},{4,6},{5,7},{6,4},{7,5},{8,10},{9,11},{10,... | collective-permute-start | bytes 1671176 | tf_op jit(solution)/shard_map/ppermute | solution.py:62
  12.7 7.6 %collective-permute-done.2.refs_3_ = bf16[128,2176]{1,0:T(8,128)(2,1)S(1)} collective-permute-done((bf16[128,2176]{1,0:T(8,128)(2,1)}, bf16[128,2176]{1,0:T(8,128)(2,1)S(1)}, u32[]{:S(2)}, u32[]{:S(2)}) %collective-permute-start.2) | collective-permute-done | bytes 557088 | tf_op jit(solution)/shard_map/ppermute | solution.py:62
  20.3 2.0 collective-permute-start.3
  22.3 9.0 %collective-permute-done.1.refs_2_ = bf16[128,2176]{1,0:T(8,128)(2,1)S(1)} collective-permute-done((bf16[128,2176]{1,0:T(8,128)(2,1)}, bf16[128,2176]{1,0:T(8,128)(2,1)S(1)}, u32[]{:S(2)}, u32[]{:S(2)}) %collective-permute-start.1) | collective-permute-done | bytes 557088 | tf_op jit(solution)/shard_map/ppermute | solution.py:62
  32.3 3.7 %pack_rows.1 = (bf16[288,2048]{1,0:T(8,128)(2,1)}, bf16[288,2048]{1,0:T(8,128)(2,1)}) custom-call(s32[1]{0:T(128)} %bitcast.6.me_ref, bf16[128,2176]{1,0:T(8,128)(2,1)} %get-tuple-element.82.refs_0_, bf16[128,2176]{1,0:T(8,128)(2,1)} %copy-done.15, bf16[128,2176]{1,0:T(8,128)(2,1)} %copy-done.13, bf16[128,2176]{1,0:T(8,128)(2,1)} %copy-done.11), custom_call_target="tpu_custom_call" | custom-call | flops 3000000000 | bytes 10000000 | tf_op jit(solution)/shard_map/pack_rows/pallas_call | solution.py:173
  36.0 2.0 collective-permute-start.9
  37.9 2.2 %collective-permute-start.10 = (bf16[288,2048]{1,0:T(8,128)(2,1)}, bf16[288,2048]{1,0:T(8,128)(2,1)S(1)}, u32[]{:S(2)}, u32[]{:S(2)}) collective-permute-start(bf16[288,2048]{1,0:T(8,128)(2,1)} %get-tuple-element.85), channel_id=1, source_target_pairs={{0,3},{1,0},{2,1},{3,2},{4,7},{5,4},{6,5},{7,6},{8,11},{9,8},{10,9... | collective-permute-start | bytes 3538952 | tf_op jit(solution)/shard_map/ppermute | solution.py:62
  41.2 4.1 %pack_scaled.1 = (bf16[288,2048]{1,0:T(8,128)(2,1)}, bf16[288,2048]{1,0:T(8,128)(2,1)}) custom-call(s32[1]{0:T(128)} %bitcast.6.me_ref, bf16[128,2176]{1,0:T(8,128)(2,1)} %get-tuple-element.75.refs_0_, bf16[128,2176]{1,0:T(8,128)(2,1)} %collective-permute-done.3.refs_1_, bf16[128,2176]{1,0:T(8,128)(2,1)} %copy-done.14, bf16[128,2176]{1,0:T(8,128)(2,1)} %copy-done.12), custom_call_target="tpu_custom_call" | custom-call | flops 3000000000 | bytes 10000000 | tf_op jit(solution)/shard_map/pack_scaled/pallas_call | solution.py:173
  48.6 3.7 %pack_rows_rest.1 = (bf16[288,2048]{1,0:T(8,128)(2,1)}, bf16[288,2048]{1,0:T(8,128)(2,1)}) custom-call(s32[1]{0:T(128)} %bitcast.6.me_ref, bf16[128,2176]{1,0:T(8,128)(2,1)} %get-tuple-element.82.refs_0_, bf16[128,2176]{1,0:T(8,128)(2,1)} %copy-done.15, bf16[128,2176]{1,0:T(8,128)(2,1)} %copy-done.13, bf16[128,2176]{1,0:T(8,128)(2,1)} %copy-done.11), custom_call_target="tpu_custom_call" | custom-call | flops 3000000000 | bytes 10000000 | tf_op jit(solution)/shard_map/pack_rows_rest/pallas_call | solution.py:173
  52.3 6.3 %up.1 = (f32[288,768]{1,0:T(8,128)}, bf16[288,768]{1,0:T(8,128)(2,1)}, bf16[288,768]{1,0:T(8,128)(2,1)}) custom-call(bf16[288,2048]{1,0:T(8,128)(2,1)} %get-tuple-element.86.refs_0_.refs_4_, bf16[2048,1536]{1,0:T(8,128)(2,1)} %bitcast.18, bf16[2048,1536]{1,0:T(8,128)(2,1)} %bitcast.19), custom_call_target="tpu_custom_call" | custom-call | flops 3000000000 | bytes 10000000 | tf_op jit(solution)/shard_map/up/pallas_call | solution.py:246
  58.6 4.1 %pack_scaled_rest.1 = (bf16[288,2048]{1,0:T(8,128)(2,1)}, bf16[288,2048]{1,0:T(8,128)(2,1)}) custom-call(s32[1]{0:T(128)} %bitcast.6.me_ref, bf16[128,2176]{1,0:T(8,128)(2,1)} %get-tuple-element.75.refs_0_, bf16[128,2176]{1,0:T(8,128)(2,1)} %collective-permute-done.3.refs_1_, bf16[128,2176]{1,0:T(8,128)(2,1)} %copy-done.14, bf16[128,2176]{1,0:T(8,128)(2,1)} %copy-done.12), custom_call_target="tpu_custom_call" | custom-call | flops 3000000000 | bytes 10000000 | tf_op jit(solution)/shard_map/pack_scaled_rest/pallas_call | solution.py:173
  62.7 3.4 %collective-permute-done.9.refs_2_.refs_5_.refs_1_ = bf16[288,2048]{1,0:T(8,128)(2,1)S(1)} collective-permute-done((bf16[288,2048]{1,0:T(8,128)(2,1)}, bf16[288,2048]{1,0:T(8,128)(2,1)S(1)}, u32[]{:S(2)}, u32[]{:S(2)}) %collective-permute-start.9) | collective-permute-done | bytes 1179680 | tf_op jit(solution)/shard_map/ppermute | solution.py:62
  66.1 2.9 %collective-permute-start.11 = (bf16[288,2048]{1,0:T(8,128)(2,1)}, bf16[288,2048]{1,0:T(8,128)(2,1)}, u32[]{:S(2)}, u32[]{:S(2)}) collective-permute-start(bf16[288,2048]{1,0:T(8,128)(2,1)} %get-tuple-element.90), channel_id=1, source_target_pairs={{0,2},{1,3},{2,0},{3,1},{4,6},{5,7},{6,4},{7,5},{8,10},{9,11},{10,... | collective-permute-start | bytes 3538952 | tf_op jit(solution)/shard_map/ppermute | solution.py:62
  69.0 4.7 %dh.1.refs_8_ = f32[288,768]{1,0:T(8,128)} custom-call(bf16[288,2048]{1,0:T(8,128)(2,1)} %get-tuple-element.80.refs_0_.refs_1_, bf16[768,2048]{1,0:T(8,128)(2,1)} %bitcast.23), custom_call_target="tpu_custom_call" | custom-call | flops 3000000000 | bytes 10000000 | tf_op jit(solution)/shard_map/dh/pallas_call | solution.py:274
  74.4 2.7 %collective-permute-start.8 = (bf16[288,2048]{1,0:T(8,128)(2,1)}, bf16[288,2048]{1,0:T(8,128)(2,1)S(1)}, u32[]{:S(2)}, u32[]{:S(2)}) collective-permute-start(bf16[288,2048]{1,0:T(8,128)(2,1)} %get-tuple-element.81), channel_id=1, source_target_pairs={{0,8},{1,9},{2,10},{3,11},{4,12},{5,13},{6,14},{7,15},{8,0},{9,1},... | collective-permute-start | bytes 3538952 | tf_op jit(solution)/shard_map/ppermute | solution.py:62
  77.1 15.8 %middle.1 = (f32[288,768]{1,0:T(8,128)}, f32[288,768]{1,0:T(8,128)}, bf16[2,3,80,768]{3,2,1,0:T(8,128)(2,1)}, f32[216,768]{1,0:T(8,128)}, bf16[16,72,2048]{2,1,0...) custom-call(s32[1]{0:T(128)} %bitcast.6.me_ref, bf16[2048,1536]{1,0:T(8,128)(2,1)} %bitcast.20, ...), custom_call_target="tpu_custom_call" | custom-call | flops 3000000000 | bytes 10000000 | tf_op jit(solution)/shard_map/middle/pallas_call | solution.py:413
  94.9 9.1 %last_x.1 = (bf16[768,1152]{1,0:T(8,128)(2,1)}, bf16[2,80,768]{2,1,0:T(8,128)(2,1)}, bf16[16,72,2048]{2,1,0:T(8,128)(2,1)}, bf16[1152,768]{1,0:T(8,128)(2,1)}, bf16[1152,768]{1,0:T(8,128)(2,1)}) custom-call(s32[1]{0:T(128)} %bitcast.6.me_ref, bf16[2048,1536]{1,0:T(8,128)(2,1)} %bitcast.21, ...), custom_call_target="tpu_custom_call", output_to_operand_aliasing={{2}: (7, {}), {3}: (8, {}), {4}: (9, {})} | custom-call | flops 3000000000 | bytes 10000000 | tf_op jit(solution)/shard_map/last_x/pallas_call | solution.py:494
  105.1 11.8 %last_s.1 = (bf16[768,512]{1,0:T(8,128)(2,1)}, bf16[768,512]{1,0:T(8,128)(2,1)}, f32[768,512]{1,0:T(8,128)}, bf16[16,72,2048]{2,1,0:T(8,128)(2,1)}, bf16[288,768]{1,0:T(8,128)(2,1)}, /*index=5*/bf16[288,768]{1,0:T(8,128)(2,1)}) custom-call(s32[1]{0:T(128)} %bitcast.6.me_ref, s32[1]{0:T(128)} %bitcast.7.place_ref, ...), custom_call_target="tpu_custom_call", output_to_operand_aliasing={{3}: (11, {})} | custom-call | flops 1 | bytes 1 | tf_op jit(solution)/shard_map/last_s/pallas_call | solution.py:618
  120.1 7.2 %all-to-all-start = ((bf16[16,72,2048]{2,1,0:T(8,128)(2,1)}), bf16[16,72,2048]{2,1,0:T(8,128)(2,1)}, u32[]{:S(2)}, u32[]{:S(2)}) async-start(bf16[16,72,2048]{2,1,0:T(8,128)(2,1)} %get-tuple-element.112), calls=%async_computation | async-start | bytes 9437184 | tf_op jit(solution)/shard_map/all_to_all | solution.py:828
  127.3 11.5 %gate_up_parts.1 = (bf16[512,1536]{1,0:T(8,128)(2,1)}, bf16[512,1536]{1,0:T(8,128)(2,1)}, f32[512,1536]{1,0:T(8,128)}, bf16[1152,768]{1,0:T(8,128)(2,1)}, bf16[1152,768]{1,0:T(8,128)(2,1)}) custom-call(s32[1]{0:T(128)} %bitcast.7.place_ref, bf16[1152,768]{1,0:T(8,128)(2,1)} %get-tuple-element.113.refs_0_, bf16[1152,768]{1,0:T(8,128)(2,1)} %get-tuple-element.114.refs_1_, ...), custom_call_target="tpu_custom_call" | custom-call | flops 1 | bytes 1 | tf_op jit(solution)/shard_map/gate_up_parts/pallas_call | solution.py:717
  139.3 2.9 %collective-permute-start.16 = (bf16[512,1536]{1,0:T(8,128)(2,1)}, bf16[512,1536]{1,0:T(8,128)(2,1)}, u32[]{:S(2)}, u32[]{:S(2)}) collective-permute-start(bf16[512,1536]{1,0:T(8,128)(2,1)} %get-tuple-element.130), channel_id=1, source_target_pairs={{0,48},{16,0},{32,16},{48,32},{1,49},{17,1},{33,17},{49,33},{2,50}... | collective-permute-start | bytes 4718600 | tf_op jit(solution)/shard_map/ppermute | solution.py:54
  142.1 6.0 %gate_up_own.1 = f32[512,1536]{1,0:T(8,128)} custom-call(s32[1]{0:T(128)} %bitcast.7.place_ref, bf16[288,2048]{1,0:T(8,128)(2,1)} %get-tuple-element.86.refs_0_.refs_4_, bf16[288,2048]{1,0:T(8,128)(2,1)} %copy-done.3, bf16[288,2048]{1,0:T(8,128)(2,1)} %copy-done.4, bf16[288,2048]{1,0:T(8,128)(2,1)} %collective-permute-done.11.refs_1_.refs_7_.refs_3_, ...), custom_call_target="tpu_custom_call" | custom-call | flops 199999995904 | bytes 10000000 | tf_op jit(solution)/shard_map/gate_up_own/pallas_call | solution.py:746
  148.2 3.9 %down_own.1 = f32[768,512]{1,0:T(8,128)} custom-call(s32[1]{0:T(128)} %bitcast.7.place_ref, bf16[768,1152]{1,0:T(8,128)(2,1)} %get-tuple-element.122.refs_0_, bf16[288,2048]{1,0:T(8,128)(2,1)} %get-tuple-element.80.refs_0_.refs_1_, bf16[288,2048]{1,0:T(8,128)(2,1)} %copy-done, bf16[288,2048]{1,0:T(8,128)(2,1)} %copy-done.1, bf16[288,2048]{1,0:T(8,128)(2,1)} %copy-done.5), custom_call_target="tpu_custom_call" | custom-call | flops 1 | bytes 1 | tf_op jit(solution)/shard_map/down_own/pallas_call | solution.py:660
  153.7 3.2 %collective-permute-start.20 = (bf16[384,512]{1,0:T(8,128)(2,1)S(1)}, bf16[384,512]{1,0:T(8,128)(2,1)S(1)}, u32[]{:S(2)}, u32[]{:S(2)}) collective-permute-start(bf16[384,512]{1,0:T(8,128)(2,1)S(1)} %get-tuple-element.142), channel_id=1, source_target_pairs={{0,48},{16,0},{32,16},{48,32},{1,49},{17,1},{33,17},{49,33},{2,50}... | collective-permute-start | bytes 1179656 | tf_op jit(solution)/shard_map/ppermute | solution.py:54
  156.9 20.8 %collective-permute-done.15 = bf16[512,1536]{1,0:T(8,128)(2,1)} collective-permute-done((bf16[512,1536]{1,0:T(8,128)(2,1)}, bf16[512,1536]{1,0:T(8,128)(2,1)}, u32[]{:S(2)}, u32[]{:S(2)}) %collective-permute-start.15) | collective-permute-done | bytes 1572896 | tf_op jit(solution)/shard_map/ppermute | solution.py:54
  177.8 2.8 %add_convert_fusion.3 = (bf16[256,1536]{1,0:T(8,128)(2,1)}, bf16[256,1536]{1,0:T(8,128)(2,1)S(1)}) fusion(f32[512,1536]{1,0:T(8,128)S(1)} %copy-done.6, bf16[512,1536]{1,0:T(8,128)(2,1)} %collective-permute-done.15, bf16[512,1536]{1,0:T(8,128)(2,1)} %collective-permute-done.16), kind=kLoop, calls=%fused_computation.4 | loop fusion | flops 2359296 | bytes 6291456 | tf_op jit(solution)/shard_map/convert_element_type | solution.py:779
  181.3 2.5 %collective-permute-start.18 = (bf16[256,1536]{1,0:T(8,128)(2,1)S(1)}, bf16[256,1536]{1,0:T(8,128)(2,1)}, u32[]{:S(2)}, u32[]{:S(2)}) collective-permute-start(bf16[256,1536]{1,0:T(8,128)(2,1)S(1)} %get-tuple-element.140), channel_id=1, source_target_pairs={{0,48},{16,0},{32,16},{48,32},{1,49},{17,1},{33,17},{49,33},{2,50}... | collective-permute-start | bytes 2359304 | tf_op jit(solution)/shard_map/ppermute | solution.py:54
  187.6 5.2 %home.1 = bf16[128,2048]{1,0:T(8,128)(2,1)} custom-call(bf16[128,128]{1,0:T(8,128)(2,1)} %get-tuple-element.71.tail_ref, bf16[1152,2048]{1,0:T(8,128)(2,1)} %bitcast.10.rows_ref, bf16[128,2048]{1,0:T(8,128)(2,1)} %bitcast.28), custom_call_target="tpu_custom_call" | custom-call | flops 3000000000 | bytes 10000000 | tf_op jit(solution)/shard_map/home/pallas_call | solution.py:210
  192.8 6.9 %collective-permute-done.17 = bf16[256,1536]{1,0:T(8,128)(2,1)} collective-permute-done((bf16[256,1536]{1,0:T(8,128)(2,1)}, bf16[256,1536]{1,0:T(8,128)(2,1)}, u32[]{:S(2)}, u32[]{:S(2)}) %collective-permute-start.17) | collective-permute-done | bytes 786464 | tf_op jit(solution)/shard_map/ppermute | solution.py:54
  199.7 3.1 %fusion = bf16[1,1,512,1536]{3,2,1,0:T(8,128)(2,1)} fusion(f32[512,1536]{1,0:T(8,128)S(1)} %copy-done.7, bf16[256,1536]{1,0:T(8,128)(2,1)S(1)} %slice.37, bf16[256,1536]{1,0:T(8,128)(2,1)S(1)} %slice.36, bf16[256,1536]{1,0:T(8,128)(2,1)} %collective-permute-done.18, bf16[256,1536]{1,0:T(8,128)(2,1)} %collective-permute-done.17), kind=kLoop, calls=%fused_computation.1 | loop fusion | flops 8650752 | bytes 7864320 | tf_op jit(solution)/shard_map/broadcast_in_dim | solution.py:847
  (69 shorter events, 22.4 us)
Async XLA Ops:
  3.0 17.3 %collective-permute-start.2 = (bf16[128,2176]{1,0:T(8,128)(2,1)}, bf16[128,2176]{1,0:T(8,128)(2,1)S(1)}, u32[]{:S(2)}, u32[]{:S(2)}) collective-permute-start(bf16[128,2176]{1,0:T(8,128)(2,1)} %get-tuple-element.82.refs_0_), channel_id=1, source_target_pairs={{0,8},{1,9},{2,10},{3,11},{4,12},{5,13},{6,14},{7,15},{8,0},{9,1},... | collective-permute-start | bytes 1671176 | tf_op jit(solution)/shard_map/ppermute | solution.py:62
  6.1 25.1 %collective-permute-start.1 = (bf16[128,2176]{1,0:T(8,128)(2,1)}, bf16[128,2176]{1,0:T(8,128)(2,1)S(1)}, u32[]{:S(2)}, u32[]{:S(2)}) collective-permute-start(bf16[128,2176]{1,0:T(8,128)(2,1)} %get-tuple-element.82.refs_0_), channel_id=1, source_target_pairs={{0,12},{1,13},{2,14},{3,15},{4,0},{5,1},{6,2},{7,3},{8,4},{9,5},{1... | collective-permute-start | bytes 1671176 | tf_op jit(solution)/shard_map/ppermute | solution.py:62
  7.2 24.0 %collective-permute-start = (bf16[128,2176]{1,0:T(8,128)(2,1)}, bf16[128,2176]{1,0:T(8,128)(2,1)S(1)}, u32[]{:S(2)}, u32[]{:S(2)}) collective-permute-start(bf16[128,2176]{1,0:T(8,128)(2,1)} %get-tuple-element.82.refs_0_), channel_id=1, source_target_pairs={{0,4},{1,5},{2,6},{3,7},{4,8},{5,9},{6,10},{7,11},{8,12},{9,13},{1... | collective-permute-start | bytes 1671176 | tf_op jit(solution)/shard_map/ppermute | solution.py:62
  8.1 32.0 %collective-permute-start.5 = (bf16[128,2176]{1,0:T(8,128)(2,1)}, bf16[128,2176]{1,0:T(8,128)(2,1)S(1)}, u32[]{:S(2)}, u32[]{:S(2)}) collective-permute-start(bf16[128,2176]{1,0:T(8,128)(2,1)} %get-tuple-element.75.refs_0_), channel_id=1, source_target_pairs={{0,2},{1,3},{2,0},{3,1},{4,6},{5,7},{6,4},{7,5},{8,10},{9,11},{10,... | collective-permute-start | bytes 1671176 | tf_op jit(solution)/shard_map/ppermute | solution.py:62
  12.0 28.2 %collective-permute-start.4 = (bf16[128,2176]{1,0:T(8,128)(2,1)}, bf16[128,2176]{1,0:T(8,128)(2,1)S(1)}, u32[]{:S(2)}, u32[]{:S(2)}) collective-permute-start(bf16[128,2176]{1,0:T(8,128)(2,1)} %get-tuple-element.75.refs_0_), channel_id=1, source_target_pairs={{0,3},{1,0},{2,1},{3,2},{4,7},{5,4},{6,5},{7,6},{8,11},{9,8},{10,9... | collective-permute-start | bytes 1671176 | tf_op jit(solution)/shard_map/ppermute | solution.py:62
  20.3 10.9 %copy-start.11 = (bf16[128,2176]{1,0:T(8,128)(2,1)}, bf16[128,2176]{1,0:T(8,128)(2,1)S(1)}, u32[]{:S(2)}) copy-start(bf16[128,2176]{1,0:T(8,128)(2,1)S(1)} %collective-permute-done.2.refs_3_) | copy-start | bytes 1671172
  20.3 19.9 %collective-permute-start.3 = (bf16[128,2176]{1,0:T(8,128)(2,1)}, bf16[128,2176]{1,0:T(8,128)(2,1)}, u32[]{:S(2)}, u32[]{:S(2)}) collective-permute-start(bf16[128,2176]{1,0:T(8,128)(2,1)} %get-tuple-element.75.refs_0_), channel_id=1, source_target_pairs={{0,1},{1,2},{2,3},{3,0},{4,5},{5,6},{6,7},{7,4},{8,9},{9,10},{10,1... | collective-permute-start | bytes 1671176 | tf_op jit(solution)/shard_map/ppermute | solution.py:62
  36.0 30.1 %collective-permute-start.9 = (bf16[288,2048]{1,0:T(8,128)(2,1)}, bf16[288,2048]{1,0:T(8,128)(2,1)S(1)}, u32[]{:S(2)}, u32[]{:S(2)}) collective-permute-start(bf16[288,2048]{1,0:T(8,128)(2,1)} %get-tuple-element.84), channel_id=1, source_target_pairs={{0,1},{1,2},{2,3},{3,0},{4,5},{5,6},{6,7},{7,4},{8,9},{9,10},{10,1... | collective-permute-start | bytes 3538952 | tf_op jit(solution)/shard_map/ppermute | solution.py:62
  37.9 28.1 %collective-permute-start.10 = (bf16[288,2048]{1,0:T(8,128)(2,1)}, bf16[288,2048]{1,0:T(8,128)(2,1)S(1)}, u32[]{:S(2)}, u32[]{:S(2)}) collective-permute-start(bf16[288,2048]{1,0:T(8,128)(2,1)} %get-tuple-element.85), channel_id=1, source_target_pairs={{0,3},{1,0},{2,1},{3,2},{4,7},{5,4},{6,5},{7,6},{8,11},{9,8},{10,9... | collective-permute-start | bytes 3538952 | tf_op jit(solution)/shard_map/ppermute | solution.py:62
  45.3 28.8 %collective-permute-start.6 = (bf16[288,2048]{1,0:T(8,128)(2,1)}, bf16[288,2048]{1,0:T(8,128)(2,1)S(1)}, u32[]{:S(2)}, u32[]{:S(2)}) collective-permute-start(bf16[288,2048]{1,0:T(8,128)(2,1)} %get-tuple-element.78), channel_id=1, source_target_pairs={{0,4},{1,5},{2,6},{3,7},{4,8},{5,9},{6,10},{7,11},{8,12},{9,13},{1... | collective-permute-start | bytes 3538952 | tf_op jit(solution)/shard_map/ppermute | solution.py:62
  46.8 27.6 %collective-permute-start.7 = (bf16[288,2048]{1,0:T(8,128)(2,1)}, bf16[288,2048]{1,0:T(8,128)(2,1)S(1)}, u32[]{:S(2)}, u32[]{:S(2)}) collective-permute-start(bf16[288,2048]{1,0:T(8,128)(2,1)} %get-tuple-element.79), channel_id=1, source_target_pairs={{0,12},{1,13},{2,14},{3,15},{4,0},{5,1},{6,2},{7,3},{8,4},{9,5},{1... | collective-permute-start | bytes 3538952 | tf_op jit(solution)/shard_map/ppermute | solution.py:62
  66.1 7.6 %copy-start.3 = (bf16[288,2048]{1,0:T(8,128)(2,1)}, bf16[288,2048]{1,0:T(8,128)(2,1)S(1)}, u32[]{:S(2)}) copy-start(bf16[288,2048]{1,0:T(8,128)(2,1)S(1)} %collective-permute-done.9.refs_2_.refs_5_.refs_1_) | copy-start | bytes 3538948
  66.1 7.6 %copy-start.4 = (bf16[288,2048]{1,0:T(8,128)(2,1)}, bf16[288,2048]{1,0:T(8,128)(2,1)S(1)}, u32[]{:S(2)}) copy-start(bf16[288,2048]{1,0:T(8,128)(2,1)S(1)} %collective-permute-done.10.refs_3_.refs_6_.refs_2_) | copy-start | bytes 3538948
  66.1 28.9 %collective-permute-start.11 = (bf16[288,2048]{1,0:T(8,128)(2,1)}, bf16[288,2048]{1,0:T(8,128)(2,1)}, u32[]{:S(2)}, u32[]{:S(2)}) collective-permute-start(bf16[288,2048]{1,0:T(8,128)(2,1)} %get-tuple-element.90), channel_id=1, source_target_pairs={{0,2},{1,3},{2,0},{3,1},{4,6},{5,7},{6,4},{7,5},{8,10},{9,11},{10,... | collective-permute-start | bytes 3538952 | tf_op jit(solution)/shard_map/ppermute | solution.py:62
  74.1 3.0 %copy-start = (bf16[288,2048]{1,0:T(8,128)(2,1)}, bf16[288,2048]{1,0:T(8,128)(2,1)S(1)}, u32[]{:S(2)}) copy-start(bf16[288,2048]{1,0:T(8,128)(2,1)S(1)} %collective-permute-done.6.refs_4_.refs_2_) | copy-start | bytes 3538948
  74.4 2.7 %copy-start.1 = (bf16[288,2048]{1,0:T(8,128)(2,1)}, bf16[288,2048]{1,0:T(8,128)(2,1)S(1)}, u32[]{:S(2)}) copy-start(bf16[288,2048]{1,0:T(8,128)(2,1)S(1)} %collective-permute-done.7.refs_5_.refs_3_) | copy-start | bytes 3538948
  74.4 29.6 %collective-permute-start.8 = (bf16[288,2048]{1,0:T(8,128)(2,1)}, bf16[288,2048]{1,0:T(8,128)(2,1)S(1)}, u32[]{:S(2)}, u32[]{:S(2)}) collective-permute-start(bf16[288,2048]{1,0:T(8,128)(2,1)} %get-tuple-element.81), channel_id=1, source_target_pairs={{0,8},{1,9},{2,10},{3,11},{4,12},{5,13},{6,14},{7,15},{8,0},{9,1},... | collective-permute-start | bytes 3538952 | tf_op jit(solution)/shard_map/ppermute | solution.py:62
  116.8 22.0 %collective-permute-start.13 = (bf16[768,512]{1,0:T(8,128)(2,1)}, bf16[768,512]{1,0:T(8,128)(2,1)S(1)}, u32[]{:S(2)}, u32[]{:S(2)}) collective-permute-start(bf16[768,512]{1,0:T(8,128)(2,1)} %get-tuple-element.127), channel_id=1, source_target_pairs={{0,16},{16,32},{32,48},{48,0},{1,17},{17,33},{33,49},{49,1},{2,18}... | collective-permute-start | bytes 2359304 | tf_op jit(solution)/shard_map/ppermute | solution.py:54
  118.5 20.3 %collective-permute-start.14 = (bf16[768,512]{1,0:T(8,128)(2,1)}, bf16[768,512]{1,0:T(8,128)(2,1)S(1)}, u32[]{:S(2)}, u32[]{:S(2)}) collective-permute-start(bf16[768,512]{1,0:T(8,128)(2,1)} %get-tuple-element.128), channel_id=1, source_target_pairs={{0,48},{16,0},{32,16},{48,32},{1,49},{17,1},{33,17},{49,33},{2,50}... | collective-permute-start | bytes 2359304 | tf_op jit(solution)/shard_map/ppermute | solution.py:54
  120.1 67.5 %all-to-all-start = ((bf16[16,72,2048]{2,1,0:T(8,128)(2,1)}), bf16[16,72,2048]{2,1,0:T(8,128)(2,1)}, u32[]{:S(2)}, u32[]{:S(2)}) async-start(bf16[16,72,2048]{2,1,0:T(8,128)(2,1)} %get-tuple-element.112), calls=%async_computation | async-start | bytes 9437184 | tf_op jit(solution)/shard_map/all_to_all | solution.py:828
  138.8 9.3 %copy-start.10 = (bf16[768,512]{1,0:T(8,128)(2,1)}, bf16[768,512]{1,0:T(8,128)(2,1)S(1)}, u32[]{:S(2)}) copy-start(bf16[768,512]{1,0:T(8,128)(2,1)S(1)} %collective-permute-done.13) | copy-start | bytes 2359300
  138.8 9.3 %copy-start.9 = (bf16[768,512]{1,0:T(8,128)(2,1)}, bf16[768,512]{1,0:T(8,128)(2,1)S(1)}, u32[]{:S(2)}) copy-start(bf16[768,512]{1,0:T(8,128)(2,1)S(1)} %collective-permute-done.14) | copy-start | bytes 2359300
  138.8 38.9 %collective-permute-start.15 = (bf16[512,1536]{1,0:T(8,128)(2,1)}, bf16[512,1536]{1,0:T(8,128)(2,1)}, u32[]{:S(2)}, u32[]{:S(2)}) collective-permute-start(bf16[512,1536]{1,0:T(8,128)(2,1)} %get-tuple-element.129), channel_id=1, source_target_pairs={{0,16},{16,32},{32,48},{48,0},{1,17},{17,33},{33,49},{49,1},{2,18}... | collective-permute-start | bytes 4718600 | tf_op jit(solution)/shard_map/ppermute | solution.py:54
  139.3 38.5 %collective-permute-start.16 = (bf16[512,1536]{1,0:T(8,128)(2,1)}, bf16[512,1536]{1,0:T(8,128)(2,1)}, u32[]{:S(2)}, u32[]{:S(2)}) collective-permute-start(bf16[512,1536]{1,0:T(8,128)(2,1)} %get-tuple-element.130), channel_id=1, source_target_pairs={{0,48},{16,0},{32,16},{48,32},{1,49},{17,1},{33,17},{49,33},{2,50}... | collective-permute-start | bytes 4718600 | tf_op jit(solution)/shard_map/ppermute | solution.py:54
  148.2 3.9 %copy-start.8 = (f32[768,512]{1,0:T(8,128)S(1)}, f32[768,512]{1,0:T(8,128)}, u32[]{:S(2)}) copy-start(f32[768,512]{1,0:T(8,128)} %get-tuple-element.138) | copy-start | bytes 4718596
  152.1 25.7 %copy-start.6 = (f32[512,1536]{1,0:T(8,128)S(1)}, f32[512,1536]{1,0:T(8,128)}, u32[]{:S(2)}) copy-start(f32[512,1536]{1,0:T(8,128)} %get-tuple-element.134) | copy-start | bytes 9437188
  153.6 32.7 %collective-permute-start.19 = (bf16[384,512]{1,0:T(8,128)(2,1)S(1)}, bf16[384,512]{1,0:T(8,128)(2,1)S(1)}, u32[]{:S(2)}, u32[]{:S(2)}) collective-permute-start(bf16[384,512]{1,0:T(8,128)(2,1)S(1)} %get-tuple-element.141), channel_id=1, source_target_pairs={{0,16},{16,32},{32,48},{48,0},{1,17},{17,33},{33,49},{49,1},{2,18}... | collective-permute-start | bytes 1179656 | tf_op jit(solution)/shard_map/ppermute | solution.py:54
  153.7 32.7 %collective-permute-start.20 = (bf16[384,512]{1,0:T(8,128)(2,1)S(1)}, bf16[384,512]{1,0:T(8,128)(2,1)S(1)}, u32[]{:S(2)}, u32[]{:S(2)}) collective-permute-start(bf16[384,512]{1,0:T(8,128)(2,1)S(1)} %get-tuple-element.142), channel_id=1, source_target_pairs={{0,48},{16,0},{32,16},{48,32},{1,49},{17,1},{33,17},{49,33},{2,50}... | collective-permute-start | bytes 1179656 | tf_op jit(solution)/shard_map/ppermute | solution.py:54
  180.6 19.1 %collective-permute-start.17 = (bf16[256,1536]{1,0:T(8,128)(2,1)}, bf16[256,1536]{1,0:T(8,128)(2,1)}, u32[]{:S(2)}, u32[]{:S(2)}) collective-permute-start(bf16[256,1536]{1,0:T(8,128)(2,1)} %get-tuple-element.139), channel_id=1, source_target_pairs={{0,16},{16,32},{32,48},{48,0},{1,17},{17,33},{33,49},{49,1},{2,18}... | collective-permute-start | bytes 2359304 | tf_op jit(solution)/shard_map/ppermute | solution.py:54
  181.3 18.3 %collective-permute-start.18 = (bf16[256,1536]{1,0:T(8,128)(2,1)S(1)}, bf16[256,1536]{1,0:T(8,128)(2,1)}, u32[]{:S(2)}, u32[]{:S(2)}) collective-permute-start(bf16[256,1536]{1,0:T(8,128)(2,1)S(1)} %get-tuple-element.140), channel_id=1, source_target_pairs={{0,48},{16,0},{32,16},{48,32},{1,49},{17,1},{33,17},{49,33},{2,50}... | collective-permute-start | bytes 2359304 | tf_op jit(solution)/shard_map/ppermute | solution.py:54
  187.6 12.0 %copy-start.7 = (f32[512,1536]{1,0:T(8,128)S(1)}, f32[512,1536]{1,0:T(8,128)}, u32[]{:S(2)}) copy-start(f32[512,1536]{1,0:T(8,128)} %gate_up_own.1) | copy-start | bytes 9437188
  192.8 10.0 %collective-permute-start.12 = (bf16[128,2048]{1,0:T(8,128)(2,1)}, bf16[128,2048]{1,0:T(8,128)(2,1)S(1)}, u32[]{:S(2)}, u32[]{:S(2)}) collective-permute-start(bf16[128,2048]{1,0:T(8,128)(2,1)} %home.1), channel_id=1, source_target_pairs={{0,64},{64,0},{1,65},{65,1},{2,66},{66,2},{3,67},{67,3},{4,68},{68... | collective-permute-start | bytes 1572872 | tf_op jit(solution)/shard_map/ppermute | solution.py:54
  (8 other events, 12.4 us)
where the time goes:
time: 204 us
  Pallas kernels  92.1 us (45%)
  waiting for transfers between devices  50.3 us (25%)
  starting transfers between devices  45.2 us (22%)
  other arithmetic  8.69 us (4%)
  local copies, waits for them, and re-layouts  6.43 us (3%)
    ppermute x9, waiting for transfers between devices, moved_along(): lax.ppermute(block, axis, [(i, (i + distance) % size) for i in range(size)])  27.7 us
    ppermute x12, starting transfers between devices, moved_along(): return lax.ppermute(block, 'expert', pairs)  24.8 us
    ppermute x12, waiting for transfers between devices, moved_along(): return lax.ppermute(block, 'expert', pairs)  22.6 us
    pallas_call x1, Pallas kernels, middle(): pl.pallas_call(functools.partial(middle_kernel, cap), in_specs=[SCALARS]...  15.8 us
    pallas_call x4, Pallas kernels, pack(): pl.pallas_call(functools.partial(pack_kernel, scale, experts, cap, steps_...  15.6 us
    ppermute x9, starting transfers between devices, moved_along(): lax.ppermute(block, axis, [(i, (i + distance) % size) for i in range(size)])  13.1 us
    pallas_call x1, Pallas kernels, last_s(): pl.pallas_call(functools.partial(last_s_kernel, cap), in_specs=[SCALARS]...  11.8 us
    pallas_call x1, Pallas kernels, gate_up_parts(): pl.pallas_call(functools.partial(gate_up_kernel, cap), in_specs=[SCALARS]...  11.5 us
  transfers between devices with their start and end apart: 22, of which 8 were waited for; matrix products, arithmetic and copies ran while one was open for 6% of the time, Pallas kernels for 38%

commit v1 on v0

--- a/solution.py
+++ b/solution.py
@@ -533,12 +533,8 @@
     for side in range(2):
         out, row = SPOTS[k][side]
         piece = part[side * half : (side + 1) * half]
-        if out == 2:
-            staged = wait_v.at[row]
-            staged[...] = piece
-        else:
-            staged = sent_v.at[out, row]
-            staged[...] = piece.astype(BF16)
+        staged = wait_v.at[row] if out == 2 else sent_v.at[out, row]
+        staged[...] = piece.astype(BF16)
         target = outs[out].at[row * half : (row + 1) * half, :]
         copies.append(begun(staged, target, sems.at[k, side]))
     return copies
@@ -550,13 +546,13 @@
 
 
 def message_outs(rows, cols):
-    return [jax.ShapeDtypeStruct((rows, cols), kind) for kind in (BF16, BF16, F32)]
+    return [jax.ShapeDtypeStruct((rows, cols), kind) for kind in (BF16, BF16, BF16)]
 
 
 def message_scratch(rows, cols):
     return [
         pltpu.VMEM((2, 2, rows // 2, cols), BF16),
-        pltpu.VMEM((2, rows // 2, cols), F32),
+        pltpu.VMEM((2, rows // 2, cols), BF16),
         pltpu.SemaphoreType.DMA((3, 2)),
     ]
 
@@ -678,32 +674,40 @@
     d_v, late_v, x_v, sent_v, wait_v, out_sems, d_sems, x_sems = refs[13:]
     rows, width = xs[0].shape
     size = width // SIDE
-    loads = []
-    for k in range(2):
-        loads.append(begun(early[k], d_v.at[k], d_sems.at[0, k]))
-        loads.append(begun(late[k], late_v.at[k], d_sems.at[1, k]))
-    for k, ahead in enumerate(AHEAD):
-        cols = ahead_of(place_ref, ahead, size)
-        for i in range(SIDE):
-            part = x_v.at[k, pl.ds(i * rows, rows), :]
-            loads.append(begun(xs[i].at[:, cols], part, x_sems.at[k, i]))
-    for load in loads[:4]:
-        load.wait()
     edge = 3 * cap - 8
-    copies = []
-    for k in range(2):
+
+    def dab_loads(k):
+        first = begun(early[k], d_v.at[k], d_sems.at[0, k])
+        return [first, begun(late[k], late_v.at[k], d_sems.at[1, k])]
+
+    def x_loads(k):
+        cols = ahead_of(place_ref, AHEAD[k], size)
+        at = [pl.ds(i * rows, rows) for i in range(SIDE)]
+        return [begun(xs[i].at[:, cols], x_v.at[k, at[i], :], x_sems.at[k, i]) for i in range(SIDE)]
+
+    def filled(k, loads):
+        for load in loads:
+            load.wait()
         fresh = late_v[k].astype(F32)
         for i in range(SIDE):
             at = slice(i * rows + edge, (i + 1) * rows)
             old = d_v[k, at, :].astype(F32)[:8]
             new = fresh[i * cap : (i + 1) * cap]
             d_v[k, at, :] = jnp.concatenate([old, new], axis=0).astype(BF16)
-        copies.append(begun(d_v.at[k], ds[k], d_sems.at[2, k]))
+        return begun(d_v.at[k], ds[k], d_sems.at[2, k])
+
+    first, quarters = dab_loads(0), [x_loads(0)]
+    second = dab_loads(1)
+    quarters += [x_loads(1), x_loads(2)]
+    copies = [filled(0, first)]
     for k in range(3):
-        for load in loads[4 * k + 4 : 4 * k + 8]:
+        for load in quarters[k]:
             load.wait()
         turned_x = x_v[k].T
-        part = jnp.concatenate([dot(turned_x, d_v[0]), dot(turned_x, d_v[1])], axis=1)
+        part = dot(turned_x, d_v[0])
+        if k == 0:
+            copies.append(filled(1, second))
+        part = jnp.concatenate([part, dot(turned_x, d_v[1])], axis=1)
         copies += put_halves(k, part, sent_v, wait_v, outs, out_sems)
     for copy in copies:
         copy.wait()
@@ -776,18 +780,19 @@
 
 def ring_second(up1, down1, first_up, first_down, wait):
     half = wait.shape[0] // 2
-    second_up = (wait[:half] + up1[:half].astype(F32)).astype(BF16)
-    second_down = (wait[half:] + down1[half:].astype(F32)).astype(BF16)
+    second_up = (wait[:half].astype(F32) + up1[:half].astype(F32)).astype(BF16)
+    second_down = (wait[half:].astype(F32) + down1[half:].astype(F32)).astype(BF16)
     return moved_along(second_up, "edata", 1), moved_along(second_down, "edata", -1)
 
 
 def ring_own(own, up1, down1):
     half = own.shape[0] // 2
-    return own + jnp.concatenate([down1[:half], up1[half:]], axis=0).astype(F32)
+    return own[:half] + down1[:half].astype(F32), own[half:] + up1[half:].astype(F32)
 
 
 def ring_last(total, up2, down2):
-    return (total + jnp.concatenate([up2, down2], axis=0).astype(F32)).astype(BF16)
+    messages = jnp.concatenate([up2, down2], axis=0).astype(F32)
+    return (jnp.concatenate(total, axis=0) + messages).astype(BF16)
 
 
 def body(hidden_in, out_grad, routes, gates, w_gate_up, w_down):
@@ -839,11 +844,15 @@
     )
     down_second = ring_second(*down_first, *down)
     gate_up_second = ring_second(*gate_up_first, *gate_up)
-    down_grad = ring_last(ring_own(own_down, *down_first), *down_second)
-    gate_up_grad = ring_last(ring_own(own_gate_up, *gate_up_first), *gate_up_second)
-
+    returned, own_down, own_gate_up, *firsts = lax.optimization_barrier(
+        (returned, own_down, own_gate_up, *down_first, *gate_up_first)
+    )
+    totals = (*ring_own(own_down, *firsts[:2]), *ring_own(own_gate_up, *firsts[2:]))
+    totals = lax.optimization_barrier(totals)
     layer = home(tail, returned.reshape(experts * cap, width), out_grad[0], experts, cap)
     upstream = moved_along(layer, "section", -1)
+    down_grad = ring_last(totals[:2], *down_second)
+    gate_up_grad = ring_last(totals[2:], *gate_up_second)
     return (upstream[None], gate_up_grad[None, None], down_grad[None, None])
 
 

time: 204 us -> 204 us (level)
  other arithmetic: 8.69 us -> 11.4 us
  local copies, waits for them, and re-layouts: 6.43 us -> 4.04 us
    ppermute x9, waiting for transfers between devices: 27.7 us -> 22.1 us  [moved_along(): lax.ppermute(block, axis, [(i, (i + distance) % size) for i in range(size)])]
    convert_element_type x2 -> x4, other arithmetic: 4.35 us -> 9.11 us  [the longest x2 5.17 us: ring_last(): return (jnp.concatenate(total, axis=0) + messages).astype(BF16)]
    all_to_all x1, waiting for transfers between devices: 0.01 us -> 4.69 us  [body(): lax.all_to_all(rows, 'expert', split_axis=0, concat_axis=0, tiled=True)]
    broadcast_in_dim x2 -> x0, other arithmetic: 4.34 us -> none  [body(): return (upstream[None], gate_up_grad[None, None], down_grad[None, None])]
    slice x6 -> x0, local copies, waits for them, and re-layouts: 2.53 us -> none  [ring_own(): return own + jnp.concatenate([down1[:half], up1[half:]], axis=0).astype(F32)]
    add x0 -> x2, other arithmetic: none -> 2.24 us  [ring_own(): own[half:] + up1[half:].astype(F32)]
  transfers between devices with their start and end apart: 22 -> 22, of which waited for: 8 -> 9; matrix products, arithmetic and copies ran while one was open for 6% -> 6% of each run, Pallas kernels for 38% -> 38%
where the time goes in v1:
time: 204 us; the launch traced here: 203 us
  Pallas kernels  91.9 us (45%)
  waiting for transfers between devices  49.4 us (24%)
  starting transfers between devices  45.4 us (22%)
  other arithmetic  11.4 us (6%)
  local copies, waits for them, and re-layouts  4.04 us (2%)
    ppermute x12, starting transfers between devices, moved_along(): return lax.ppermute(block, 'expert', pairs)  25 us
    ppermute x12, waiting for transfers between devices, moved_along(): return lax.ppermute(block, 'expert', pairs)  22.6 us
    ppermute x9, waiting for transfers between devices, moved_along(): lax.ppermute(block, axis, [(i, (i + distance) % size) for i in range(size)])  22.1 us
    pallas_call x1, Pallas kernels, middle(): pl.pallas_call(functools.partial(middle_kernel, cap), in_specs=[SCALARS]...  15.8 us
    pallas_call x4, Pallas kernels, pack(): pl.pallas_call(functools.partial(pack_kernel, scale, experts, cap, steps_...  15.6 us
    ppermute x9, starting transfers between devices, moved_along(): lax.ppermute(block, axis, [(i, (i + distance) % size) for i in range(size)])  13.3 us
    pallas_call x1, Pallas kernels, last_s(): pl.pallas_call(functools.partial(last_s_kernel, cap), in_specs=[SCALARS]...  11.7 us
    pallas_call x1, Pallas kernels, gate_up_parts(): pl.pallas_call(functools.partial(gate_up_kernel, cap), in_specs=[SCALARS]...  11.2 us
  transfers between devices with their start and end apart: 22, of which 9 were waited for; matrix products, arithmetic and copies ran while one was open for 6% of the time, Pallas kernels for 38%

profile of v1, /device:TPU:0, one launch (start us, length us, event | category | flops | bytes accessed | tf_op | source)
XLA Modules:
  0.0 203.0 jit_solution(8000422546942194645)
XLA Ops:
  0.6 2.4 %prep.1 = (bf16[128,2176]{1,0:T(8,128)(2,1)}, bf16[128,2176]{1,0:T(8,128)(2,1)}, bf16[128,128]{1,0:T(8,128)(2,1)}) custom-call(s32[8,128]{1,0:T(8,128)} %bitcast.39, f32[8,128]{1,0:T(8,128)} %bitcast.40, bf16[128,2048]{1,0:T(8,128)(2,1)} %bitcast.35, bf16[128,2048]{1,0:T(8,128)(2,1)} %bitcast.36), custom_call_target="tpu_custom_call" | custom-call | tf_op jit(solution)/shard_map/prep/pallas_call | solution.py:97
  3.0 3.1 %collective-permute-start.2 = (bf16[128,2176]{1,0:T(8,128)(2,1)}, bf16[128,2176]{1,0:T(8,128)(2,1)S(1)}, u32[]{:S(2)}, u32[]{:S(2)}) collective-permute-start(bf16[128,2176]{1,0:T(8,128)(2,1)} %get-tuple-element.93.refs_0_), channel_id=1, source_target_pairs={{0,8},{1,9},{2,10},{3,11},{4,12},{5,13},{6,14},{7,15},{8,0},{9,1},... | collective-permute-start | bytes 1671176 | tf_op jit(solution)/shard_map/ppermute | solution.py:62
  8.1 3.9 %collective-permute-start.5 = (bf16[128,2176]{1,0:T(8,128)(2,1)}, bf16[128,2176]{1,0:T(8,128)(2,1)S(1)}, u32[]{:S(2)}, u32[]{:S(2)}) collective-permute-start(bf16[128,2176]{1,0:T(8,128)(2,1)} %get-tuple-element.86.refs_0_), channel_id=1, source_target_pairs={{0,2},{1,3},{2,0},{3,1},{4,6},{5,7},{6,4},{7,5},{8,10},{9,11},{10,... | collective-permute-start | bytes 1671176 | tf_op jit(solution)/shard_map/ppermute | solution.py:62
  12.7 7.6 %collective-permute-done.2.refs_3_ = bf16[128,2176]{1,0:T(8,128)(2,1)S(1)} collective-permute-done((bf16[128,2176]{1,0:T(8,128)(2,1)}, bf16[128,2176]{1,0:T(8,128)(2,1)S(1)}, u32[]{:S(2)}, u32[]{:S(2)}) %collective-permute-start.2) | collective-permute-done | bytes 557088 | tf_op jit(solution)/shard_map/ppermute | solution.py:62
  22.3 9.0 %collective-permute-done.1.refs_2_ = bf16[128,2176]{1,0:T(8,128)(2,1)S(1)} collective-permute-done((bf16[128,2176]{1,0:T(8,128)(2,1)}, bf16[128,2176]{1,0:T(8,128)(2,1)S(1)}, u32[]{:S(2)}, u32[]{:S(2)}) %collective-permute-start.1) | collective-permute-done | bytes 557088 | tf_op jit(solution)/shard_map/ppermute | solution.py:62
  32.2 3.7 %pack_rows.1 = (bf16[288,2048]{1,0:T(8,128)(2,1)}, bf16[288,2048]{1,0:T(8,128)(2,1)}) custom-call(s32[1]{0:T(128)} %bitcast.6.me_ref, bf16[128,2176]{1,0:T(8,128)(2,1)} %get-tuple-element.93.refs_0_, bf16[128,2176]{1,0:T(8,128)(2,1)} %copy-done.17, bf16[128,2176]{1,0:T(8,128)(2,1)} %copy-done.15, bf16[128,2176]{1,0:T(8,128)(2,1)} %copy-done.13), custom_call_target="tpu_custom_call" | custom-call | flops 3000000000 | bytes 10000000 | tf_op jit(solution)/shard_map/pack_rows/pallas_call | solution.py:173
  38.0 2.2 %collective-permute-start.10 = (bf16[288,2048]{1,0:T(8,128)(2,1)}, bf16[288,2048]{1,0:T(8,128)(2,1)S(1)}, u32[]{:S(2)}, u32[]{:S(2)}) collective-permute-start(bf16[288,2048]{1,0:T(8,128)(2,1)} %get-tuple-element.96), channel_id=1, source_target_pairs={{0,3},{1,0},{2,1},{3,2},{4,7},{5,4},{6,5},{7,6},{8,11},{9,8},{10,9... | collective-permute-start | bytes 3538952 | tf_op jit(solution)/shard_map/ppermute | solution.py:62
  41.2 4.1 %pack_scaled.1 = (bf16[288,2048]{1,0:T(8,128)(2,1)}, bf16[288,2048]{1,0:T(8,128)(2,1)}) custom-call(s32[1]{0:T(128)} %bitcast.6.me_ref, bf16[128,2176]{1,0:T(8,128)(2,1)} %get-tuple-element.86.refs_0_, bf16[128,2176]{1,0:T(8,128)(2,1)} %collective-permute-done.3.refs_1_, bf16[128,2176]{1,0:T(8,128)(2,1)} %copy-done.16, bf16[128,2176]{1,0:T(8,128)(2,1)} %copy-done.14), custom_call_target="tpu_custom_call" | custom-call | flops 3000000000 | bytes 10000000 | tf_op jit(solution)/shard_map/pack_scaled/pallas_call | solution.py:173
  48.6 3.7 %pack_rows_rest.1 = (bf16[288,2048]{1,0:T(8,128)(2,1)}, bf16[288,2048]{1,0:T(8,128)(2,1)}) custom-call(s32[1]{0:T(128)} %bitcast.6.me_ref, bf16[128,2176]{1,0:T(8,128)(2,1)} %get-tuple-element.93.refs_0_, bf16[128,2176]{1,0:T(8,128)(2,1)} %copy-done.17, bf16[128,2176]{1,0:T(8,128)(2,1)} %copy-done.15, bf16[128,2176]{1,0:T(8,128)(2,1)} %copy-done.13), custom_call_target="tpu_custom_call" | custom-call | flops 3000000000 | bytes 10000000 | tf_op jit(solution)/shard_map/pack_rows_rest/pallas_call | solution.py:173
  52.2 6.3 %up.1 = (f32[288,768]{1,0:T(8,128)}, bf16[288,768]{1,0:T(8,128)(2,1)}, bf16[288,768]{1,0:T(8,128)(2,1)}) custom-call(bf16[288,2048]{1,0:T(8,128)(2,1)} %get-tuple-element.97.refs_0_.refs_4_, bf16[2048,1536]{1,0:T(8,128)(2,1)} %bitcast.22, bf16[2048,1536]{1,0:T(8,128)(2,1)} %bitcast.23), custom_call_target="tpu_custom_call" | custom-call | flops 3000000000 | bytes 10000000 | tf_op jit(solution)/shard_map/up/pallas_call | solution.py:246
  58.5 4.1 %pack_scaled_rest.1 = (bf16[288,2048]{1,0:T(8,128)(2,1)}, bf16[288,2048]{1,0:T(8,128)(2,1)}) custom-call(s32[1]{0:T(128)} %bitcast.6.me_ref, bf16[128,2176]{1,0:T(8,128)(2,1)} %get-tuple-element.86.refs_0_, bf16[128,2176]{1,0:T(8,128)(2,1)} %collective-permute-done.3.refs_1_, bf16[128,2176]{1,0:T(8,128)(2,1)} %copy-done.16, bf16[128,2176]{1,0:T(8,128)(2,1)} %copy-done.14), custom_call_target="tpu_custom_call" | custom-call | flops 3000000000 | bytes 10000000 | tf_op jit(solution)/shard_map/pack_scaled_rest/pallas_call | solution.py:173
  62.7 3.4 %collective-permute-done.9.refs_2_.refs_5_.refs_1_ = bf16[288,2048]{1,0:T(8,128)(2,1)S(1)} collective-permute-done((bf16[288,2048]{1,0:T(8,128)(2,1)}, bf16[288,2048]{1,0:T(8,128)(2,1)S(1)}, u32[]{:S(2)}, u32[]{:S(2)}) %collective-permute-start.9) | collective-permute-done | bytes 1179680 | tf_op jit(solution)/shard_map/ppermute | solution.py:62
  66.1 2.9 %collective-permute-start.11 = (bf16[288,2048]{1,0:T(8,128)(2,1)}, bf16[288,2048]{1,0:T(8,128)(2,1)}, u32[]{:S(2)}, u32[]{:S(2)}) collective-permute-start(bf16[288,2048]{1,0:T(8,128)(2,1)} %get-tuple-element.101), channel_id=1, source_target_pairs={{0,2},{1,3},{2,0},{3,1},{4,6},{5,7},{6,4},{7,5},{8,10},{9,11},{10,... | collective-permute-start | bytes 3538952 | tf_op jit(solution)/shard_map/ppermute | solution.py:62
  69.0 4.7 %dh.1.refs_8_ = f32[288,768]{1,0:T(8,128)} custom-call(bf16[288,2048]{1,0:T(8,128)(2,1)} %get-tuple-element.91.refs_0_.refs_1_, bf16[768,2048]{1,0:T(8,128)(2,1)} %bitcast.27), custom_call_target="tpu_custom_call" | custom-call | flops 3000000000 | bytes 10000000 | tf_op jit(solution)/shard_map/dh/pallas_call | solution.py:274
  74.3 2.9 %collective-permute-start.8 = (bf16[288,2048]{1,0:T(8,128)(2,1)}, bf16[288,2048]{1,0:T(8,128)(2,1)S(1)}, u32[]{:S(2)}, u32[]{:S(2)}) collective-permute-start(bf16[288,2048]{1,0:T(8,128)(2,1)} %get-tuple-element.92), channel_id=1, source_target_pairs={{0,8},{1,9},{2,10},{3,11},{4,12},{5,13},{6,14},{7,15},{8,0},{9,1},... | collective-permute-start | bytes 3538952 | tf_op jit(solution)/shard_map/ppermute | solution.py:62
  77.2 15.8 %middle.1 = (f32[288,768]{1,0:T(8,128)}, f32[288,768]{1,0:T(8,128)}, bf16[2,3,80,768]{3,2,1,0:T(8,128)(2,1)}, f32[216,768]{1,0:T(8,128)}, bf16[16,72,2048]{2,1,0...) custom-call(s32[1]{0:T(128)} %bitcast.6.me_ref, bf16[2048,1536]{1,0:T(8,128)(2,1)} %bitcast.24, ...), custom_call_target="tpu_custom_call" | custom-call | flops 3000000000 | bytes 10000000 | tf_op jit(solution)/shard_map/middle/pallas_call | solution.py:413
  93.0 2.0 collective-permute-done.11.refs_1_.refs_7_.refs_3_
  95.0 9.1 %last_x.1 = (bf16[768,1152]{1,0:T(8,128)(2,1)}, bf16[2,80,768]{2,1,0:T(8,128)(2,1)}, bf16[16,72,2048]{2,1,0:T(8,128)(2,1)}, bf16[1152,768]{1,0:T(8,128)(2,1)}, bf16[1152,768]{1,0:T(8,128)(2,1)}) custom-call(s32[1]{0:T(128)} %bitcast.6.me_ref, bf16[2048,1536]{1,0:T(8,128)(2,1)} %bitcast.25, ...), custom_call_target="tpu_custom_call", output_to_operand_aliasing={{2}: (7, {}), {3}: (8, {}), {4}: (9, {})} | custom-call | flops 3000000000 | bytes 10000000 | tf_op jit(solution)/shard_map/last_x/pallas_call | solution.py:494
  105.1 11.7 %last_s.1 = (bf16[768,512]{1,0:T(8,128)(2,1)}, bf16[768,512]{1,0:T(8,128)(2,1)}, bf16[768,512]{1,0:T(8,128)(2,1)}, bf16[16,72,2048]{2,1,0:T(8,128)(2,1)}, bf16[2...) custom-call(s32[1]{0:T(128)} %bitcast.6.me_ref, s32[1]{0:T(128)} %bitcast.7.place_ref, ...), custom_call_target="tpu_custom_call", output_to_operand_aliasing={{3}: (11, {})} | custom-call | flops 1 | bytes 1 | tf_op jit(solution)/shard_map/last_s/pallas_call | solution.py:614
  120.2 7.1 %all-to-all-start = ((bf16[16,72,2048]{2,1,0:T(8,128)(2,1)}), bf16[16,72,2048]{2,1,0:T(8,128)(2,1)}, u32[]{:S(2)}, u32[]{:S(2)}) async-start(bf16[16,72,2048]{2,1,0:T(8,128)(2,1)} %get-tuple-element.123), calls=%async_computation | async-start | bytes 9437184 | tf_op jit(solution)/shard_map/all_to_all | solution.py:833
  127.3 11.2 %gate_up_parts.1 = (bf16[512,1536]{1,0:T(8,128)(2,1)}, bf16[512,1536]{1,0:T(8,128)(2,1)}, bf16[512,1536]{1,0:T(8,128)(2,1)}, bf16[1152,768]{1,0:T(8,128)(2,1)}, bf16[1152,768]{1,0:T(8,128)(2,1)}) custom-call(s32[1]{0:T(128)} %bitcast.7.place_ref, bf16[1152,768]{1,0:T(8,128)(2,1)} %get-tuple-element.124.refs_0_, ...), custom_call_target="tpu_custom_call" | custom-call | flops 1 | bytes 1 | tf_op jit(solution)/shard_map/gate_up_parts/pallas_call | solution.py:721
  139.0 2.9 %collective-permute-start.15 = (bf16[512,1536]{1,0:T(8,128)(2,1)}, bf16[512,1536]{1,0:T(8,128)(2,1)}, u32[]{:S(2)}, u32[]{:S(2)}) collective-permute-start(bf16[512,1536]{1,0:T(8,128)(2,1)} %get-tuple-element.141), channel_id=1, source_target_pairs={{0,48},{16,0},{32,16},{48,32},{1,49},{17,1},{33,17},{49,33},{2,50}... | collective-permute-start | bytes 4718600 | tf_op jit(solution)/shard_map/ppermute | solution.py:54
  141.9 6.1 %gate_up_own.1 = f32[512,1536]{1,0:T(8,128)} custom-call(s32[1]{0:T(128)} %bitcast.7.place_ref, bf16[288,2048]{1,0:T(8,128)(2,1)} %get-tuple-element.97.refs_0_.refs_4_, bf16[288,2048]{1,0:T(8,128)(2,1)} %copy-done.3, bf16[288,2048]{1,0:T(8,128)(2,1)} %copy-done.4, bf16[288,2048]{1,0:T(8,128)(2,1)} %collective-permute-done.11.refs_1_.refs_7_.refs_3_, ...), custom_call_target="tpu_custom_call" | custom-call | flops 199999995904 | bytes 10000000 | tf_op jit(solution)/shard_map/gate_up_own/pallas_call | solution.py:750
  148.0 3.9 %down_own.1 = f32[768,512]{1,0:T(8,128)} custom-call(s32[1]{0:T(128)} %bitcast.7.place_ref, bf16[768,1152]{1,0:T(8,128)(2,1)} %get-tuple-element.133.refs_0_, bf16[288,2048]{1,0:T(8,128)(2,1)} %get-tuple-element.91.refs_0_.refs_1_, bf16[288,2048]{1,0:T(8,128)(2,1)} %copy-done, bf16[288,2048]{1,0:T(8,128)(2,1)} %copy-done.1, bf16[288,2048]{1,0:T(8,128)(2,1)} %copy-done.5), custom_call_target="tpu_custom_call" | custom-call | flops 1 | bytes 1 | tf_op jit(solution)/shard_map/down_own/pallas_call | solution.py:656
  151.9 2.2 %add_convert_fusion.3 = (bf16[384,512]{1,0:T(8,128)(2,1)}, bf16[384,512]{1,0:T(8,128)(2,1)S(1)}) fusion(bf16[768,512]{1,0:T(8,128)(2,1)} %copy-done.9, bf16[768,512]{1,0:T(8,128)(2,1)S(1)} %copy-done.8, bf16[768,512]{1,0:T(8,128)(2,1)} %copy-done.11), kind=kLoop, calls=%fused_computation.9 | loop fusion | flops 1572864 | bytes 2359296 | tf_op jit(solution)/shard_map/convert_element_type | solution.py:783
  154.1 3.2 %collective-permute-start.20 = (bf16[384,512]{1,0:T(8,128)(2,1)S(1)}, bf16[384,512]{1,0:T(8,128)(2,1)}, u32[]{:S(2)}, u32[]{:S(2)}) collective-permute-start(bf16[384,512]{1,0:T(8,128)(2,1)S(1)} %get-tuple-element.168), channel_id=1, source_target_pairs={{0,48},{16,0},{32,16},{48,32},{1,49},{17,1},{33,17},{49,33},{2,50}... | collective-permute-start | bytes 1179656 | tf_op jit(solution)/shard_map/ppermute | solution.py:54
  157.3 20.2 %collective-permute-done.14 = bf16[512,1536]{1,0:T(8,128)(2,1)} collective-permute-done((bf16[512,1536]{1,0:T(8,128)(2,1)}, bf16[512,1536]{1,0:T(8,128)(2,1)}, u32[]{:S(2)}, u32[]{:S(2)}) %collective-permute-start.14) | collective-permute-done | bytes 1572896 | tf_op jit(solution)/shard_map/ppermute | solution.py:54
  180.0 2.6 %collective-permute-start.18 = (bf16[256,1536]{1,0:T(8,128)(2,1)S(1)}, bf16[256,1536]{1,0:T(8,128)(2,1)}, u32[]{:S(2)}, u32[]{:S(2)}) collective-permute-start(bf16[256,1536]{1,0:T(8,128)(2,1)S(1)} %get-tuple-element.164), channel_id=1, source_target_pairs={{0,48},{16,0},{32,16},{48,32},{1,49},{17,1},{33,17},{49,33},{2,50}... | collective-permute-start | bytes 2359304 | tf_op jit(solution)/shard_map/ppermute | solution.py:54
  182.6 4.7 %all-to-all-done = bf16[16,72,2048]{2,1,0:T(8,128)(2,1)} async-done(((bf16[16,72,2048]{2,1,0:T(8,128)(2,1)}), bf16[16,72,2048]{2,1,0:T(8,128)(2,1)}, u32[]{:S(2)}, u32[]{:S(2)}) %all-to-all-start) | async-done | bytes 4718624 | tf_op jit(solution)/shard_map/all_to_all | solution.py:833
  187.3 5.1 %home.1 = bf16[128,2048]{1,0:T(8,128)(2,1)} custom-call(bf16[128,128]{1,0:T(8,128)(2,1)} %get-tuple-element.82.tail_ref, bf16[1152,2048]{1,0:T(8,128)(2,1)} %bitcast.10.rows_ref, bf16[128,2048]{1,0:T(8,128)(2,1)} %bitcast.37), custom_call_target="tpu_custom_call" | custom-call | flops 3000000000 | bytes 10000000 | tf_op jit(solution)/shard_map/home/pallas_call | solution.py:210
  195.1 2.3 %fusion.1 = bf16[1,1,768,512]{3,2,1,0:T(8,128)(2,1)} fusion(f32[1,1,384,512]{3,2,1,0:T(8,128)S(1)} %bitcast.32, f32[1,1,384,512]{3,2,1,0:T(8,128)S(1)} %bitcast.33, bf16[1,1,384,512]{3,2,1,0:T(8,128)(2,1)} %bitcast.19, bf16[1,1,384,512]{3,2,1,0:T(8,128)(2,1)} %bitcast.18), kind=kLoop, calls=%fused_computation.3 | loop fusion | flops 2752512 | bytes 3145728 | tf_op jit(solution)/shard_map/convert_element_type | solution.py:795
  199.3 2.9 %fusion = bf16[1,1,512,1536]{3,2,1,0:T(8,128)(2,1)} fusion(f32[1,1,256,1536]{3,2,1,0:T(8,128)S(1)} %bitcast.30, f32[1,1,256,1536]{3,2,1,0:T(8,128)S(1)} %bitcast.31, bf16[1,1,256,1536]{3,2,1,0:T(8,128)(2,1)} %bitcast.15, bf16[1,1,256,1536]{3,2,1,0:T(8,128)(2,1)S(1)} %bitcast.34), kind=kLoop, calls=%fused_computation.1 | loop fusion | flops 5505024 | bytes 6291456 | tf_op jit(solution)/shard_map/convert_element_type | solution.py:795
  (69 shorter events, 25.2 us)
Async XLA Ops:
  3.0 17.3 %collective-permute-start.2 = (bf16[128,2176]{1,0:T(8,128)(2,1)}, bf16[128,2176]{1,0:T(8,128)(2,1)S(1)}, u32[]{:S(2)}, u32[]{:S(2)}) collective-permute-start(bf16[128,2176]{1,0:T(8,128)(2,1)} %get-tuple-element.93.refs_0_), channel_id=1, source_target_pairs={{0,8},{1,9},{2,10},{3,11},{4,12},{5,13},{6,14},{7,15},{8,0},{9,1},... | collective-permute-start | bytes 1671176 | tf_op jit(solution)/shard_map/ppermute | solution.py:62
  6.1 25.1 %collective-permute-start.1 = (bf16[128,2176]{1,0:T(8,128)(2,1)}, bf16[128,2176]{1,0:T(8,128)(2,1)S(1)}, u32[]{:S(2)}, u32[]{:S(2)}) collective-permute-start(bf16[128,2176]{1,0:T(8,128)(2,1)} %get-tuple-element.93.refs_0_), channel_id=1, source_target_pairs={{0,12},{1,13},{2,14},{3,15},{4,0},{5,1},{6,2},{7,3},{8,4},{9,5},{1... | collective-permute-start | bytes 1671176 | tf_op jit(solution)/shard_map/ppermute | solution.py:62
  7.2 24.0 %collective-permute-start = (bf16[128,2176]{1,0:T(8,128)(2,1)}, bf16[128,2176]{1,0:T(8,128)(2,1)S(1)}, u32[]{:S(2)}, u32[]{:S(2)}) collective-permute-start(bf16[128,2176]{1,0:T(8,128)(2,1)} %get-tuple-element.93.refs_0_), channel_id=1, source_target_pairs={{0,4},{1,5},{2,6},{3,7},{4,8},{5,9},{6,10},{7,11},{8,12},{9,13},{1... | collective-permute-start | bytes 1671176 | tf_op jit(solution)/shard_map/ppermute | solution.py:62
  8.1 32.0 %collective-permute-start.5 = (bf16[128,2176]{1,0:T(8,128)(2,1)}, bf16[128,2176]{1,0:T(8,128)(2,1)S(1)}, u32[]{:S(2)}, u32[]{:S(2)}) collective-permute-start(bf16[128,2176]{1,0:T(8,128)(2,1)} %get-tuple-element.86.refs_0_), channel_id=1, source_target_pairs={{0,2},{1,3},{2,0},{3,1},{4,6},{5,7},{6,4},{7,5},{8,10},{9,11},{10,... | collective-permute-start | bytes 1671176 | tf_op jit(solution)/shard_map/ppermute | solution.py:62
  12.0 28.2 %collective-permute-start.4 = (bf16[128,2176]{1,0:T(8,128)(2,1)}, bf16[128,2176]{1,0:T(8,128)(2,1)S(1)}, u32[]{:S(2)}, u32[]{:S(2)}) collective-permute-start(bf16[128,2176]{1,0:T(8,128)(2,1)} %get-tuple-element.86.refs_0_), channel_id=1, source_target_pairs={{0,3},{1,0},{2,1},{3,2},{4,7},{5,4},{6,5},{7,6},{8,11},{9,8},{10,9... | collective-permute-start | bytes 1671176 | tf_op jit(solution)/shard_map/ppermute | solution.py:62
  20.3 10.9 %copy-start.13 = (bf16[128,2176]{1,0:T(8,128)(2,1)}, bf16[128,2176]{1,0:T(8,128)(2,1)S(1)}, u32[]{:S(2)}) copy-start(bf16[128,2176]{1,0:T(8,128)(2,1)S(1)} %collective-permute-done.2.refs_3_) | copy-start | bytes 1671172
  20.3 19.9 %collective-permute-start.3 = (bf16[128,2176]{1,0:T(8,128)(2,1)}, bf16[128,2176]{1,0:T(8,128)(2,1)}, u32[]{:S(2)}, u32[]{:S(2)}) collective-permute-start(bf16[128,2176]{1,0:T(8,128)(2,1)} %get-tuple-element.86.refs_0_), channel_id=1, source_target_pairs={{0,1},{1,2},{2,3},{3,0},{4,5},{5,6},{6,7},{7,4},{8,9},{9,10},{10,1... | collective-permute-start | bytes 1671176 | tf_op jit(solution)/shard_map/ppermute | solution.py:62
  36.0 30.1 %collective-permute-start.9 = (bf16[288,2048]{1,0:T(8,128)(2,1)}, bf16[288,2048]{1,0:T(8,128)(2,1)S(1)}, u32[]{:S(2)}, u32[]{:S(2)}) collective-permute-start(bf16[288,2048]{1,0:T(8,128)(2,1)} %get-tuple-element.95), channel_id=1, source_target_pairs={{0,1},{1,2},{2,3},{3,0},{4,5},{5,6},{6,7},{7,4},{8,9},{9,10},{10,1... | collective-permute-start | bytes 3538952 | tf_op jit(solution)/shard_map/ppermute | solution.py:62
  38.0 28.2 %collective-permute-start.10 = (bf16[288,2048]{1,0:T(8,128)(2,1)}, bf16[288,2048]{1,0:T(8,128)(2,1)S(1)}, u32[]{:S(2)}, u32[]{:S(2)}) collective-permute-start(bf16[288,2048]{1,0:T(8,128)(2,1)} %get-tuple-element.96), channel_id=1, source_target_pairs={{0,3},{1,0},{2,1},{3,2},{4,7},{5,4},{6,5},{7,6},{8,11},{9,8},{10,9... | collective-permute-start | bytes 3538952 | tf_op jit(solution)/shard_map/ppermute | solution.py:62
  45.3 28.8 %collective-permute-start.6 = (bf16[288,2048]{1,0:T(8,128)(2,1)}, bf16[288,2048]{1,0:T(8,128)(2,1)S(1)}, u32[]{:S(2)}, u32[]{:S(2)}) collective-permute-start(bf16[288,2048]{1,0:T(8,128)(2,1)} %get-tuple-element.89), channel_id=1, source_target_pairs={{0,4},{1,5},{2,6},{3,7},{4,8},{5,9},{6,10},{7,11},{8,12},{9,13},{1... | collective-permute-start | bytes 3538952 | tf_op jit(solution)/shard_map/ppermute | solution.py:62
  46.7 27.6 %collective-permute-start.7 = (bf16[288,2048]{1,0:T(8,128)(2,1)}, bf16[288,2048]{1,0:T(8,128)(2,1)S(1)}, u32[]{:S(2)}, u32[]{:S(2)}) collective-permute-start(bf16[288,2048]{1,0:T(8,128)(2,1)} %get-tuple-element.90), channel_id=1, source_target_pairs={{0,12},{1,13},{2,14},{3,15},{4,0},{5,1},{6,2},{7,3},{8,4},{9,5},{1... | collective-permute-start | bytes 3538952 | tf_op jit(solution)/shard_map/ppermute | solution.py:62
  66.1 7.7 %copy-start.3 = (bf16[288,2048]{1,0:T(8,128)(2,1)}, bf16[288,2048]{1,0:T(8,128)(2,1)S(1)}, u32[]{:S(2)}) copy-start(bf16[288,2048]{1,0:T(8,128)(2,1)S(1)} %collective-permute-done.9.refs_2_.refs_5_.refs_1_) | copy-start | bytes 3538948
  66.1 7.7 %copy-start.4 = (bf16[288,2048]{1,0:T(8,128)(2,1)}, bf16[288,2048]{1,0:T(8,128)(2,1)S(1)}, u32[]{:S(2)}) copy-start(bf16[288,2048]{1,0:T(8,128)(2,1)S(1)} %collective-permute-done.10.refs_3_.refs_6_.refs_2_) | copy-start | bytes 3538948
  66.1 28.9 %collective-permute-start.11 = (bf16[288,2048]{1,0:T(8,128)(2,1)}, bf16[288,2048]{1,0:T(8,128)(2,1)}, u32[]{:S(2)}, u32[]{:S(2)}) collective-permute-start(bf16[288,2048]{1,0:T(8,128)(2,1)} %get-tuple-element.101), channel_id=1, source_target_pairs={{0,2},{1,3},{2,0},{3,1},{4,6},{5,7},{6,4},{7,5},{8,10},{9,11},{10,... | collective-permute-start | bytes 3538952 | tf_op jit(solution)/shard_map/ppermute | solution.py:62
  74.0 3.2 %copy-start = (bf16[288,2048]{1,0:T(8,128)(2,1)}, bf16[288,2048]{1,0:T(8,128)(2,1)S(1)}, u32[]{:S(2)}) copy-start(bf16[288,2048]{1,0:T(8,128)(2,1)S(1)} %collective-permute-done.6.refs_4_.refs_2_) | copy-start | bytes 3538948
  74.3 2.9 %copy-start.1 = (bf16[288,2048]{1,0:T(8,128)(2,1)}, bf16[288,2048]{1,0:T(8,128)(2,1)S(1)}, u32[]{:S(2)}) copy-start(bf16[288,2048]{1,0:T(8,128)(2,1)S(1)} %collective-permute-done.7.refs_5_.refs_3_) | copy-start | bytes 3538948
  74.3 29.8 %collective-permute-start.8 = (bf16[288,2048]{1,0:T(8,128)(2,1)}, bf16[288,2048]{1,0:T(8,128)(2,1)S(1)}, u32[]{:S(2)}, u32[]{:S(2)}) collective-permute-start(bf16[288,2048]{1,0:T(8,128)(2,1)} %get-tuple-element.92), channel_id=1, source_target_pairs={{0,8},{1,9},{2,10},{3,11},{4,12},{5,13},{6,14},{7,15},{8,0},{9,1},... | collective-permute-start | bytes 3538952 | tf_op jit(solution)/shard_map/ppermute | solution.py:62
  116.8 21.7 %collective-permute-start.12 = (bf16[768,512]{1,0:T(8,128)(2,1)}, bf16[768,512]{1,0:T(8,128)(2,1)S(1)}, u32[]{:S(2)}, u32[]{:S(2)}) collective-permute-start(bf16[768,512]{1,0:T(8,128)(2,1)} %get-tuple-element.138), channel_id=1, source_target_pairs={{0,16},{16,32},{32,48},{48,0},{1,17},{17,33},{33,49},{49,1},{2,18}... | collective-permute-start | bytes 2359304 | tf_op jit(solution)/shard_map/ppermute | solution.py:54
  118.5 20.0 %collective-permute-start.13 = (bf16[768,512]{1,0:T(8,128)(2,1)}, bf16[768,512]{1,0:T(8,128)(2,1)S(1)}, u32[]{:S(2)}, u32[]{:S(2)}) collective-permute-start(bf16[768,512]{1,0:T(8,128)(2,1)} %get-tuple-element.139), channel_id=1, source_target_pairs={{0,48},{16,0},{32,16},{48,32},{1,49},{17,1},{33,17},{49,33},{2,50}... | collective-permute-start | bytes 2359304 | tf_op jit(solution)/shard_map/ppermute | solution.py:54
  120.2 67.2 %all-to-all-start = ((bf16[16,72,2048]{2,1,0:T(8,128)(2,1)}), bf16[16,72,2048]{2,1,0:T(8,128)(2,1)}, u32[]{:S(2)}, u32[]{:S(2)}) async-start(bf16[16,72,2048]{2,1,0:T(8,128)(2,1)} %get-tuple-element.123), calls=%async_computation | async-start | bytes 9437184 | tf_op jit(solution)/shard_map/all_to_all | solution.py:833
  138.5 9.5 %copy-start.9 = (bf16[768,512]{1,0:T(8,128)(2,1)}, bf16[768,512]{1,0:T(8,128)(2,1)S(1)}, u32[]{:S(2)}) copy-start(bf16[768,512]{1,0:T(8,128)(2,1)S(1)} %collective-permute-done.12) | copy-start | bytes 2359300
  138.5 9.4 %copy-start.11 = (bf16[768,512]{1,0:T(8,128)(2,1)}, bf16[768,512]{1,0:T(8,128)(2,1)S(1)}, u32[]{:S(2)}) copy-start(bf16[768,512]{1,0:T(8,128)(2,1)S(1)} %collective-permute-done.13) | copy-start | bytes 2359300
  138.5 38.9 %collective-permute-start.14 = (bf16[512,1536]{1,0:T(8,128)(2,1)}, bf16[512,1536]{1,0:T(8,128)(2,1)}, u32[]{:S(2)}, u32[]{:S(2)}) collective-permute-start(bf16[512,1536]{1,0:T(8,128)(2,1)} %get-tuple-element.140), channel_id=1, source_target_pairs={{0,16},{16,32},{32,48},{48,0},{1,17},{17,33},{33,49},{49,1},{2,18}... | collective-permute-start | bytes 4718600 | tf_op jit(solution)/shard_map/ppermute | solution.py:54
  139.0 38.5 %collective-permute-start.15 = (bf16[512,1536]{1,0:T(8,128)(2,1)}, bf16[512,1536]{1,0:T(8,128)(2,1)}, u32[]{:S(2)}, u32[]{:S(2)}) collective-permute-start(bf16[512,1536]{1,0:T(8,128)(2,1)} %get-tuple-element.141), channel_id=1, source_target_pairs={{0,48},{16,0},{32,16},{48,32},{1,49},{17,1},{33,17},{49,33},{2,50}... | collective-permute-start | bytes 4718600 | tf_op jit(solution)/shard_map/ppermute | solution.py:54
  148.0 3.9 %copy-start.8 = (bf16[768,512]{1,0:T(8,128)(2,1)S(1)}, bf16[768,512]{1,0:T(8,128)(2,1)}, u32[]{:S(2)}) copy-start(bf16[768,512]{1,0:T(8,128)(2,1)} %get-tuple-element.160) | copy-start | bytes 2359300
  151.9 25.6 %copy-start.7 = (bf16[512,1536]{1,0:T(8,128)(2,1)S(1)}, bf16[512,1536]{1,0:T(8,128)(2,1)}, u32[]{:S(2)}) copy-start(bf16[512,1536]{1,0:T(8,128)(2,1)} %get-tuple-element.157) | copy-start | bytes 4718596
  154.1 41.0 %collective-permute-start.19 = (bf16[384,512]{1,0:T(8,128)(2,1)}, bf16[384,512]{1,0:T(8,128)(2,1)}, u32[]{:S(2)}, u32[]{:S(2)}) collective-permute-start(bf16[384,512]{1,0:T(8,128)(2,1)} %get-tuple-element.167), channel_id=1, source_target_pairs={{0,16},{16,32},{32,48},{48,0},{1,17},{17,33},{33,49},{49,1},{2,18}... | collective-permute-start | bytes 1179656 | tf_op jit(solution)/shard_map/ppermute | solution.py:54
  154.1 41.0 %collective-permute-start.20 = (bf16[384,512]{1,0:T(8,128)(2,1)S(1)}, bf16[384,512]{1,0:T(8,128)(2,1)}, u32[]{:S(2)}, u32[]{:S(2)}) collective-permute-start(bf16[384,512]{1,0:T(8,128)(2,1)S(1)} %get-tuple-element.168), channel_id=1, source_target_pairs={{0,48},{16,0},{32,16},{48,32},{1,49},{17,1},{33,17},{49,33},{2,50}... | collective-permute-start | bytes 1179656 | tf_op jit(solution)/shard_map/ppermute | solution.py:54
  179.2 20.1 %collective-permute-start.17 = (bf16[256,1536]{1,0:T(8,128)(2,1)S(1)}, bf16[256,1536]{1,0:T(8,128)(2,1)S(1)}, u32[]{:S(2)}, u32[]{:S(2)}) collective-permute-start(bf16[256,1536]{1,0:T(8,128)(2,1)S(1)} %get-tuple-element.163), channel_id=1, source_target_pairs={{0,16},{16,32},{32,48},{48,0},{1,17},{17,33},{33,49},{49,1},{2,18}... | collective-permute-start | bytes 2359304 | tf_op jit(solution)/shard_map/ppermute | solution.py:54
  180.0 19.3 %collective-permute-start.18 = (bf16[256,1536]{1,0:T(8,128)(2,1)S(1)}, bf16[256,1536]{1,0:T(8,128)(2,1)}, u32[]{:S(2)}, u32[]{:S(2)}) collective-permute-start(bf16[256,1536]{1,0:T(8,128)(2,1)S(1)} %get-tuple-element.164), channel_id=1, source_target_pairs={{0,48},{16,0},{32,16},{48,32},{1,49},{17,1},{33,17},{49,33},{2,50}... | collective-permute-start | bytes 2359304 | tf_op jit(solution)/shard_map/ppermute | solution.py:54
  187.3 5.3 %copy-start.6 = (f32[512,1536]{1,0:T(8,128)S(1)}, f32[512,1536]{1,0:T(8,128)}, u32[]{:S(2)}) copy-start(f32[512,1536]{1,0:T(8,128)} %gate_up_own.1) | copy-start | bytes 9437188
  192.5 9.7 %collective-permute-start.16 = (bf16[128,2048]{1,0:T(8,128)(2,1)}, bf16[128,2048]{1,0:T(8,128)(2,1)S(1)}, u32[]{:S(2)}, u32[]{:S(2)}) collective-permute-start(bf16[128,2048]{1,0:T(8,128)(2,1)} %home.1), channel_id=1, source_target_pairs={{0,64},{64,0},{1,65},{65,1},{2,66},{66,2},{3,67},{67,3},{4,68},{68... | collective-permute-start | bytes 1572872 | tf_op jit(solution)/shard_map/ppermute | solution.py:54
  (8 other events, 11.2 us)

commit v2 on v1

--- a/solution.py
+++ b/solution.py
@@ -232,8 +232,8 @@
         b = dot(rows, wb[...])
         sig = jax.nn.sigmoid(a)
         outs[3 * i][...] = a * sig * b
-        outs[3 * i + 1][...] = (b * sig * (1.0 + a * (1.0 - sig))).astype(BF16)
-        outs[3 * i + 2][...] = (a * sig).astype(BF16)
+        outs[3 * i + 1][...] = b * sig * (1.0 + a * (1.0 - sig))
+        outs[3 * i + 2][...] = a * sig
 
 
 def up(xs, wgu):
@@ -242,7 +242,6 @@
     hidden = wgu.shape[1] // 2
     step = 256
     steps = hidden // step
-    kinds = (F32, BF16, BF16) * count
     flat = pl.pallas_call(
         functools.partial(up_kernel, count),
         grid=(steps,),
@@ -252,7 +251,7 @@
             pl.BlockSpec((width, step), lambda i: (0, i + steps)),
         ],
         out_specs=[pl.BlockSpec((rows, step), lambda i: (0, i))] * (3 * count),
-        out_shape=[jax.ShapeDtypeStruct((rows, hidden), kind) for kind in kinds],
+        out_shape=[jax.ShapeDtypeStruct((rows, hidden), F32)] * (3 * count),
         compiler_params=params(1),
         cost_estimate=cost(3e9, 10e6),
         name="up",
@@ -362,7 +361,7 @@
             h, factors = activations(x_v[n], w_v, t, hidden)
             h_v[n, :, tile(t, 256)] = h
             for k in range(2):
-                f_v[k, n + 1, :, tile(t, 256)] = factors[k].astype(BF16)
+                f_v[k, n + 1, :, tile(t, 256)] = factors[k]
 
     copies = [begun(h_v.at[n], h_out[n], out_sems.at[n]) for n in range(2)]
     for load in s_loads:
@@ -388,7 +387,7 @@
             chunks = [dh_v[j, :, cols] for j in range(3)]
             kept = []
             for i in range(3):
-                factor = f_v[k, i, :, cols].astype(F32)[: 3 * cap]
+                factor = f_v[k, i, :, cols][: 3 * cap]
                 product = crossed(chunks, i, cap) * factor
                 kept.append(product)
                 whole = jnp.concatenate([product, jnp.zeros((cap, 256), F32)], axis=0)
@@ -407,7 +406,7 @@
     hidden = wdown.shape[0]
     steps = width // 512
     h = jax.ShapeDtypeStruct((rows, hidden), F32)
-    tail = jax.ShapeDtypeStruct((2, 3, cap + 8, hidden), BF16)
+    tail = jax.ShapeDtypeStruct((2, 3, cap + 8, hidden), F32)
     dab = jax.ShapeDtypeStruct((SIDE * rows, hidden), BF16)
     slots = jax.ShapeDtypeStruct((SIDE * SIDE, cap, width), BF16)
     h1, h2, tails, dh_tail, slots, da, db = pl.pallas_call(
@@ -421,9 +420,9 @@
             pltpu.VMEM((2, rows, width), BF16),
             pltpu.VMEM((2, rows, width), BF16),
             pltpu.VMEM((2, rows, hidden), F32),
-            pltpu.VMEM((2, 3, rows, hidden), BF16),
+            pltpu.VMEM((2, 3, rows, hidden), F32),
             pltpu.VMEM((3, rows, hidden), F32),
-            pltpu.VMEM((2, 3, cap + 8, hidden), BF16),
+            pltpu.VMEM((2, 3, cap + 8, hidden), F32),
             pltpu.VMEM((3 * cap, hidden), F32),
             pltpu.VMEM((2, 3 * rows, hidden), BF16),
             pltpu.VMEM((2, 9 * cap, hidden), BF16),
@@ -461,7 +460,7 @@
         h, factors = activations(x_v[...], w_v, t, hidden)
         h_v[3, :, tile(t, 256)] = h
         for k in range(2):
-            f_v[k, :, tile(t, 256)] = factors[k].astype(BF16)
+            f_v[k, :, tile(t, 256)] = factors[k]
 
     for load in loads:
         load.wait()
@@ -473,7 +472,7 @@
         whole = jnp.concatenate([crossed(parts, j, cap) for j in range(SIDE)], axis=0)
         turned_v[cols, :] = whole.T.astype(BF16)
         for k in range(2):
-            product = dh_v[:, cols] * f_v[k, :, cols].astype(F32)[: 3 * cap]
+            product = dh_v[:, cols] * f_v[k, :, cols][: 3 * cap]
             e_v[k, :, cols] = product.astype(BF16)
             whole = jnp.concatenate([product, jnp.zeros((cap, 256), F32)], axis=0)
             d_v[k, :, cols] = whole.astype(BF16)
@@ -497,7 +496,7 @@
         out_specs=[FAR] * 5,
         out_shape=[
             jax.ShapeDtypeStruct((hidden, SIDE * rows), BF16),
-            jax.ShapeDtypeStruct((2, cap + 8, hidden), BF16),
+            jax.ShapeDtypeStruct((2, cap + 8, hidden), F32),
         ]
         + [jax.ShapeDtypeStruct(a.shape, BF16) for a in (slots, *ds)],
         input_output_aliases={7: 2, 8: 3, 9: 4},
@@ -505,7 +504,7 @@
             pltpu.VMEM((width, 2 * hidden), BF16),
             pltpu.VMEM((rows, width), BF16),
             pltpu.VMEM((SIDE, rows, hidden), F32),
-            pltpu.VMEM((2, rows, hidden), BF16),
+            pltpu.VMEM((2, rows, hidden), F32),
             pltpu.VMEM((3 * cap, hidden), F32),
             pltpu.VMEM((hidden, SIDE * rows), BF16),
             pltpu.VMEM((2, rows, hidden), BF16),
@@ -594,7 +593,7 @@
         cols = tile(t, 256)
         dh = dot(s_v[...], wd_v[cols, :], 1, 1)
         for k in range(2):
-            factors = [f_v[k, i, :, cols].astype(F32)[8:] for i in range(SIDE)]
+            factors = [f_v[k, i, :, cols][8:] for i in range(SIDE)]
             d_v[k, :, cols] = (dh * jnp.concatenate(factors, axis=0)).astype(BF16)
 
     copies += [begun(d_v.at[k], ds[k], out_sems.at[k]) for k in range(2)]
@@ -623,7 +622,7 @@
             pltpu.VMEM((3, total, quarter), BF16),
             pltpu.VMEM((rows, width), BF16),
             pltpu.VMEM((hidden, width), BF16),
-            pltpu.VMEM((2, SIDE, cap + 8, hidden), BF16),
+            pltpu.VMEM((2, SIDE, cap + 8, hidden), F32),
             pltpu.VMEM((2, rows, hidden), BF16),
             pltpu.VMEM((width, 2 * hidden), BF16),
             pltpu.VMEM((steps, SIDE, cap, 512), BF16),

time: 204 us -> 204 us (level)
  transfers between devices with their start and end apart: 22 -> 22, of which waited for: 9 -> 9; matrix products, arithmetic and copies ran while one was open for 6% -> 6% of each run, Pallas kernels for 38% -> 39%
where the time goes in v2:
time: 204 us; the launch traced here: 203 us
  Pallas kernels  93.5 us (46%)
  waiting for transfers between devices  48.4 us (24%)
  starting transfers between devices  45.3 us (22%)
  other arithmetic  11.4 us (6%)
  local copies, waits for them, and re-layouts  4.06 us (2%)
    ppermute x12, starting transfers between devices, moved_along(): return lax.ppermute(block, 'expert', pairs)  24.9 us
    ppermute x9, waiting for transfers between devices, moved_along(): lax.ppermute(block, axis, [(i, (i + distance) % size) for i in range(size)])  22.1 us
    ppermute x12, waiting for transfers between devices, moved_along(): return lax.ppermute(block, 'expert', pairs)  21.6 us
    pallas_call x1, Pallas kernels, middle(): pl.pallas_call(functools.partial(middle_kernel, cap), in_specs=[SCALARS]...  16 us
    pallas_call x4, Pallas kernels, pack(): pl.pallas_call(functools.partial(pack_kernel, scale, experts, cap, steps_...  15.6 us
    ppermute x9, starting transfers between devices, moved_along(): lax.ppermute(block, axis, [(i, (i + distance) % size) for i in range(size)])  13.3 us
    pallas_call x1, Pallas kernels, last_s(): pl.pallas_call(functools.partial(last_s_kernel, cap), in_specs=[SCALARS]...  12.2 us
    pallas_call x1, Pallas kernels, gate_up_parts(): pl.pallas_call(functools.partial(gate_up_kernel, cap), in_specs=[SCALARS]...  11.2 us
  transfers between devices with their start and end apart: 22, of which 9 were waited for; matrix products, arithmetic and copies ran while one was open for 6% of the time, Pallas kernels for 39%

profile of v2, /device:TPU:0, one launch (start us, length us, event | category | flops | bytes accessed | tf_op | source)
XLA Modules:
  0.0 203.4 jit_solution(1877630641628863165)
XLA Ops:
  0.6 2.4 %prep.1 = (bf16[128,2176]{1,0:T(8,128)(2,1)}, bf16[128,2176]{1,0:T(8,128)(2,1)}, bf16[128,128]{1,0:T(8,128)(2,1)}) custom-call(s32[8,128]{1,0:T(8,128)} %bitcast.39, f32[8,128]{1,0:T(8,128)} %bitcast.40, bf16[128,2048]{1,0:T(8,128)(2,1)} %bitcast.35, bf16[128,2048]{1,0:T(8,128)(2,1)} %bitcast.36), custom_call_target="tpu_custom_call" | custom-call | tf_op jit(solution)/shard_map/prep/pallas_call | solution.py:97
  3.0 3.1 %collective-permute-start.2 = (bf16[128,2176]{1,0:T(8,128)(2,1)}, bf16[128,2176]{1,0:T(8,128)(2,1)S(1)}, u32[]{:S(2)}, u32[]{:S(2)}) collective-permute-start(bf16[128,2176]{1,0:T(8,128)(2,1)} %get-tuple-element.93.refs_0_), channel_id=1, source_target_pairs={{0,8},{1,9},{2,10},{3,11},{4,12},{5,13},{6,14},{7,15},{8,0},{9,1},... | collective-permute-start | bytes 1671176 | tf_op jit(solution)/shard_map/ppermute | solution.py:62
  8.1 3.9 %collective-permute-start.5 = (bf16[128,2176]{1,0:T(8,128)(2,1)}, bf16[128,2176]{1,0:T(8,128)(2,1)S(1)}, u32[]{:S(2)}, u32[]{:S(2)}) collective-permute-start(bf16[128,2176]{1,0:T(8,128)(2,1)} %get-tuple-element.86.refs_0_), channel_id=1, source_target_pairs={{0,2},{1,3},{2,0},{3,1},{4,6},{5,7},{6,4},{7,5},{8,10},{9,11},{10,... | collective-permute-start | bytes 1671176 | tf_op jit(solution)/shard_map/ppermute | solution.py:62
  12.7 7.6 %collective-permute-done.2.refs_3_ = bf16[128,2176]{1,0:T(8,128)(2,1)S(1)} collective-permute-done((bf16[128,2176]{1,0:T(8,128)(2,1)}, bf16[128,2176]{1,0:T(8,128)(2,1)S(1)}, u32[]{:S(2)}, u32[]{:S(2)}) %collective-permute-start.2) | collective-permute-done | bytes 557088 | tf_op jit(solution)/shard_map/ppermute | solution.py:62
  22.3 9.0 %collective-permute-done.1.refs_2_ = bf16[128,2176]{1,0:T(8,128)(2,1)S(1)} collective-permute-done((bf16[128,2176]{1,0:T(8,128)(2,1)}, bf16[128,2176]{1,0:T(8,128)(2,1)S(1)}, u32[]{:S(2)}, u32[]{:S(2)}) %collective-permute-start.1) | collective-permute-done | bytes 557088 | tf_op jit(solution)/shard_map/ppermute | solution.py:62
  32.2 3.7 %pack_rows.1 = (bf16[288,2048]{1,0:T(8,128)(2,1)}, bf16[288,2048]{1,0:T(8,128)(2,1)}) custom-call(s32[1]{0:T(128)} %bitcast.6.me_ref, bf16[128,2176]{1,0:T(8,128)(2,1)} %get-tuple-element.93.refs_0_, bf16[128,2176]{1,0:T(8,128)(2,1)} %copy-done.17, bf16[128,2176]{1,0:T(8,128)(2,1)} %copy-done.15, bf16[128,2176]{1,0:T(8,128)(2,1)} %copy-done.13), custom_call_target="tpu_custom_call" | custom-call | flops 3000000000 | bytes 10000000 | tf_op jit(solution)/shard_map/pack_rows/pallas_call | solution.py:173
  36.0 2.0 collective-permute-start.9
  37.9 2.2 %collective-permute-start.10 = (bf16[288,2048]{1,0:T(8,128)(2,1)}, bf16[288,2048]{1,0:T(8,128)(2,1)S(1)}, u32[]{:S(2)}, u32[]{:S(2)}) collective-permute-start(bf16[288,2048]{1,0:T(8,128)(2,1)} %get-tuple-element.96), channel_id=1, source_target_pairs={{0,3},{1,0},{2,1},{3,2},{4,7},{5,4},{6,5},{7,6},{8,11},{9,8},{10,9... | collective-permute-start | bytes 3538952 | tf_op jit(solution)/shard_map/ppermute | solution.py:62
  41.2 4.1 %pack_scaled.1 = (bf16[288,2048]{1,0:T(8,128)(2,1)}, bf16[288,2048]{1,0:T(8,128)(2,1)}) custom-call(s32[1]{0:T(128)} %bitcast.6.me_ref, bf16[128,2176]{1,0:T(8,128)(2,1)} %get-tuple-element.86.refs_0_, bf16[128,2176]{1,0:T(8,128)(2,1)} %collective-permute-done.3.refs_1_, bf16[128,2176]{1,0:T(8,128)(2,1)} %copy-done.16, bf16[128,2176]{1,0:T(8,128)(2,1)} %copy-done.14), custom_call_target="tpu_custom_call" | custom-call | flops 3000000000 | bytes 10000000 | tf_op jit(solution)/shard_map/pack_scaled/pallas_call | solution.py:173
  48.6 3.7 %pack_rows_rest.1 = (bf16[288,2048]{1,0:T(8,128)(2,1)}, bf16[288,2048]{1,0:T(8,128)(2,1)}) custom-call(s32[1]{0:T(128)} %bitcast.6.me_ref, bf16[128,2176]{1,0:T(8,128)(2,1)} %get-tuple-element.93.refs_0_, bf16[128,2176]{1,0:T(8,128)(2,1)} %copy-done.17, bf16[128,2176]{1,0:T(8,128)(2,1)} %copy-done.15, bf16[128,2176]{1,0:T(8,128)(2,1)} %copy-done.13), custom_call_target="tpu_custom_call" | custom-call | flops 3000000000 | bytes 10000000 | tf_op jit(solution)/shard_map/pack_rows_rest/pallas_call | solution.py:173
  52.3 7.1 %up.1 = (f32[288,768]{1,0:T(8,128)}, f32[288,768]{1,0:T(8,128)}, f32[288,768]{1,0:T(8,128)}) custom-call(bf16[288,2048]{1,0:T(8,128)(2,1)} %get-tuple-element.97.refs_0_.refs_4_, bf16[2048,1536]{1,0:T(8,128)(2,1)} %bitcast.22, bf16[2048,1536]{1,0:T(8,128)(2,1)} %bitcast.23), custom_call_target="tpu_custom_call" | custom-call | flops 3000000000 | bytes 10000000 | tf_op jit(solution)/shard_map/up/pallas_call | solution.py:245
  59.4 4.1 %pack_scaled_rest.1 = (bf16[288,2048]{1,0:T(8,128)(2,1)}, bf16[288,2048]{1,0:T(8,128)(2,1)}) custom-call(s32[1]{0:T(128)} %bitcast.6.me_ref, bf16[128,2176]{1,0:T(8,128)(2,1)} %get-tuple-element.86.refs_0_, bf16[128,2176]{1,0:T(8,128)(2,1)} %collective-permute-done.3.refs_1_, bf16[128,2176]{1,0:T(8,128)(2,1)} %copy-done.16, bf16[128,2176]{1,0:T(8,128)(2,1)} %copy-done.14), custom_call_target="tpu_custom_call" | custom-call | flops 3000000000 | bytes 10000000 | tf_op jit(solution)/shard_map/pack_scaled_rest/pallas_call | solution.py:173
  63.6 2.5 %collective-permute-done.9.refs_2_.refs_5_.refs_1_ = bf16[288,2048]{1,0:T(8,128)(2,1)S(1)} collective-permute-done((bf16[288,2048]{1,0:T(8,128)(2,1)}, bf16[288,2048]{1,0:T(8,128)(2,1)S(1)}, u32[]{:S(2)}, u32[]{:S(2)}) %collective-permute-start.9) | collective-permute-done | bytes 1179680 | tf_op jit(solution)/shard_map/ppermute | solution.py:62
  66.1 2.9 %collective-permute-start.11 = (bf16[288,2048]{1,0:T(8,128)(2,1)}, bf16[288,2048]{1,0:T(8,128)(2,1)}, u32[]{:S(2)}, u32[]{:S(2)}) collective-permute-start(bf16[288,2048]{1,0:T(8,128)(2,1)} %get-tuple-element.101), channel_id=1, source_target_pairs={{0,2},{1,3},{2,0},{3,1},{4,6},{5,7},{6,4},{7,5},{8,10},{9,11},{10,... | collective-permute-start | bytes 3538952 | tf_op jit(solution)/shard_map/ppermute | solution.py:62
  69.0 4.7 %dh.1.refs_8_ = f32[288,768]{1,0:T(8,128)} custom-call(bf16[288,2048]{1,0:T(8,128)(2,1)} %get-tuple-element.91.refs_0_.refs_1_, bf16[768,2048]{1,0:T(8,128)(2,1)} %bitcast.27), custom_call_target="tpu_custom_call" | custom-call | flops 3000000000 | bytes 10000000 | tf_op jit(solution)/shard_map/dh/pallas_call | solution.py:273
  74.4 2.8 %collective-permute-start.8 = (bf16[288,2048]{1,0:T(8,128)(2,1)}, bf16[288,2048]{1,0:T(8,128)(2,1)S(1)}, u32[]{:S(2)}, u32[]{:S(2)}) collective-permute-start(bf16[288,2048]{1,0:T(8,128)(2,1)} %get-tuple-element.92), channel_id=1, source_target_pairs={{0,8},{1,9},{2,10},{3,11},{4,12},{5,13},{6,14},{7,15},{8,0},{9,1},... | collective-permute-start | bytes 3538952 | tf_op jit(solution)/shard_map/ppermute | solution.py:62
  77.1 16.0 %middle.1 = (f32[288,768]{1,0:T(8,128)}, f32[288,768]{1,0:T(8,128)}, f32[2,3,80,768]{3,2,1,0:T(8,128)}, f32[216,768]{1,0:T(8,128)}, bf16[16,72,2048]{2,1,0:T(8,1...) custom-call(s32[1]{0:T(128)} %bitcast.6.me_ref, bf16[2048,1536]{1,0:T(8,128)(2,1)} %bitcast.24, ...), custom_call_target="tpu_custom_call" | custom-call | flops 3000000000 | bytes 10000000 | tf_op jit(solution)/shard_map/middle/pallas_call | solution.py:412
  95.0 9.1 %last_x.1 = (bf16[768,1152]{1,0:T(8,128)(2,1)}, f32[2,80,768]{2,1,0:T(8,128)}, bf16[16,72,2048]{2,1,0:T(8,128)(2,1)}, bf16[1152,768]{1,0:T(8,128)(2,1)}, bf16[1152,768]{1,0:T(8,128)(2,1)}) custom-call(s32[1]{0:T(128)} %bitcast.6.me_ref, bf16[2048,1536]{1,0:T(8,128)(2,1)} %bitcast.25, ...), custom_call_target="tpu_custom_call", output_to_operand_aliasing={{2}: (7, {}), {3}: (8, {}), {4}: (9, {})} | custom-call | flops 3000000000 | bytes 10000000 | tf_op jit(solution)/shard_map/last_x/pallas_call | solution.py:493
  105.1 12.2 %last_s.1 = (bf16[768,512]{1,0:T(8,128)(2,1)}, bf16[768,512]{1,0:T(8,128)(2,1)}, bf16[768,512]{1,0:T(8,128)(2,1)}, bf16[16,72,2048]{2,1,0:T(8,128)(2,1)}, bf16[2...) custom-call(s32[1]{0:T(128)} %bitcast.6.me_ref, s32[1]{0:T(128)} %bitcast.7.place_ref, ...), custom_call_target="tpu_custom_call", output_to_operand_aliasing={{3}: (11, {})} | custom-call | flops 1 | bytes 1 | tf_op jit(solution)/shard_map/last_s/pallas_call | solution.py:613
  120.6 7.1 %all-to-all-start = ((bf16[16,72,2048]{2,1,0:T(8,128)(2,1)}), bf16[16,72,2048]{2,1,0:T(8,128)(2,1)}, u32[]{:S(2)}, u32[]{:S(2)}) async-start(bf16[16,72,2048]{2,1,0:T(8,128)(2,1)} %get-tuple-element.123), calls=%async_computation | async-start | bytes 9437184 | tf_op jit(solution)/shard_map/all_to_all | solution.py:832
  127.7 11.2 %gate_up_parts.1 = (bf16[512,1536]{1,0:T(8,128)(2,1)}, bf16[512,1536]{1,0:T(8,128)(2,1)}, bf16[512,1536]{1,0:T(8,128)(2,1)}, bf16[1152,768]{1,0:T(8,128)(2,1)}, bf16[1152,768]{1,0:T(8,128)(2,1)}) custom-call(s32[1]{0:T(128)} %bitcast.7.place_ref, bf16[1152,768]{1,0:T(8,128)(2,1)} %get-tuple-element.124.refs_0_, ...), custom_call_target="tpu_custom_call" | custom-call | flops 1 | bytes 1 | tf_op jit(solution)/shard_map/gate_up_parts/pallas_call | solution.py:720
  139.5 2.9 %collective-permute-start.15 = (bf16[512,1536]{1,0:T(8,128)(2,1)}, bf16[512,1536]{1,0:T(8,128)(2,1)}, u32[]{:S(2)}, u32[]{:S(2)}) collective-permute-start(bf16[512,1536]{1,0:T(8,128)(2,1)} %get-tuple-element.141), channel_id=1, source_target_pairs={{0,48},{16,0},{32,16},{48,32},{1,49},{17,1},{33,17},{49,33},{2,50}... | collective-permute-start | bytes 4718600 | tf_op jit(solution)/shard_map/ppermute | solution.py:54
  142.3 6.1 %gate_up_own.1 = f32[512,1536]{1,0:T(8,128)} custom-call(s32[1]{0:T(128)} %bitcast.7.place_ref, bf16[288,2048]{1,0:T(8,128)(2,1)} %get-tuple-element.97.refs_0_.refs_4_, bf16[288,2048]{1,0:T(8,128)(2,1)} %copy-done.3, bf16[288,2048]{1,0:T(8,128)(2,1)} %copy-done.4, bf16[288,2048]{1,0:T(8,128)(2,1)} %collective-permute-done.11.refs_1_.refs_7_.refs_3_, ...), custom_call_target="tpu_custom_call" | custom-call | flops 199999995904 | bytes 10000000 | tf_op jit(solution)/shard_map/gate_up_own/pallas_call | solution.py:749
  148.5 3.9 %down_own.1 = f32[768,512]{1,0:T(8,128)} custom-call(s32[1]{0:T(128)} %bitcast.7.place_ref, bf16[768,1152]{1,0:T(8,128)(2,1)} %get-tuple-element.133.refs_0_, bf16[288,2048]{1,0:T(8,128)(2,1)} %get-tuple-element.91.refs_0_.refs_1_, bf16[288,2048]{1,0:T(8,128)(2,1)} %copy-done, bf16[288,2048]{1,0:T(8,128)(2,1)} %copy-done.1, bf16[288,2048]{1,0:T(8,128)(2,1)} %copy-done.5), custom_call_target="tpu_custom_call" | custom-call | flops 1 | bytes 1 | tf_op jit(solution)/shard_map/down_own/pallas_call | solution.py:655
  152.3 2.2 %add_convert_fusion.3 = (bf16[384,512]{1,0:T(8,128)(2,1)}, bf16[384,512]{1,0:T(8,128)(2,1)S(1)}) fusion(bf16[768,512]{1,0:T(8,128)(2,1)} %copy-done.9, bf16[768,512]{1,0:T(8,128)(2,1)S(1)} %copy-done.8, bf16[768,512]{1,0:T(8,128)(2,1)} %copy-done.11), kind=kLoop, calls=%fused_computation.9 | loop fusion | flops 1572864 | bytes 2359296 | tf_op jit(solution)/shard_map/convert_element_type | solution.py:782
  154.5 3.2 %collective-permute-start.20 = (bf16[384,512]{1,0:T(8,128)(2,1)S(1)}, bf16[384,512]{1,0:T(8,128)(2,1)}, u32[]{:S(2)}, u32[]{:S(2)}) collective-permute-start(bf16[384,512]{1,0:T(8,128)(2,1)S(1)} %get-tuple-element.168), channel_id=1, source_target_pairs={{0,48},{16,0},{32,16},{48,32},{1,49},{17,1},{33,17},{49,33},{2,50}... | collective-permute-start | bytes 1179656 | tf_op jit(solution)/shard_map/ppermute | solution.py:54
  157.8 20.2 %collective-permute-done.14 = bf16[512,1536]{1,0:T(8,128)(2,1)} collective-permute-done((bf16[512,1536]{1,0:T(8,128)(2,1)}, bf16[512,1536]{1,0:T(8,128)(2,1)}, u32[]{:S(2)}, u32[]{:S(2)}) %collective-permute-start.14) | collective-permute-done | bytes 1572896 | tf_op jit(solution)/shard_map/ppermute | solution.py:54
  180.5 2.6 %collective-permute-start.18 = (bf16[256,1536]{1,0:T(8,128)(2,1)S(1)}, bf16[256,1536]{1,0:T(8,128)(2,1)}, u32[]{:S(2)}, u32[]{:S(2)}) collective-permute-start(bf16[256,1536]{1,0:T(8,128)(2,1)S(1)} %get-tuple-element.164), channel_id=1, source_target_pairs={{0,48},{16,0},{32,16},{48,32},{1,49},{17,1},{33,17},{49,33},{2,50}... | collective-permute-start | bytes 2359304 | tf_op jit(solution)/shard_map/ppermute | solution.py:54
  183.1 4.7 %all-to-all-done = bf16[16,72,2048]{2,1,0:T(8,128)(2,1)} async-done(((bf16[16,72,2048]{2,1,0:T(8,128)(2,1)}), bf16[16,72,2048]{2,1,0:T(8,128)(2,1)}, u32[]{:S(2)}, u32[]{:S(2)}) %all-to-all-start) | async-done | bytes 4718624 | tf_op jit(solution)/shard_map/all_to_all | solution.py:832
  187.8 5.2 %home.1 = bf16[128,2048]{1,0:T(8,128)(2,1)} custom-call(bf16[128,128]{1,0:T(8,128)(2,1)} %get-tuple-element.82.tail_ref, bf16[1152,2048]{1,0:T(8,128)(2,1)} %bitcast.10.rows_ref, bf16[128,2048]{1,0:T(8,128)(2,1)} %bitcast.37), custom_call_target="tpu_custom_call" | custom-call | flops 3000000000 | bytes 10000000 | tf_op jit(solution)/shard_map/home/pallas_call | solution.py:210
  195.5 2.3 %fusion.1 = bf16[1,1,768,512]{3,2,1,0:T(8,128)(2,1)} fusion(f32[1,1,384,512]{3,2,1,0:T(8,128)S(1)} %bitcast.32, f32[1,1,384,512]{3,2,1,0:T(8,128)S(1)} %bitcast.33, bf16[1,1,384,512]{3,2,1,0:T(8,128)(2,1)} %bitcast.19, bf16[1,1,384,512]{3,2,1,0:T(8,128)(2,1)} %bitcast.18), kind=kLoop, calls=%fused_computation.3 | loop fusion | flops 2752512 | bytes 3145728 | tf_op jit(solution)/shard_map/convert_element_type | solution.py:794
  199.8 2.9 %fusion = bf16[1,1,512,1536]{3,2,1,0:T(8,128)(2,1)} fusion(f32[1,1,256,1536]{3,2,1,0:T(8,128)S(1)} %bitcast.30, f32[1,1,256,1536]{3,2,1,0:T(8,128)S(1)} %bitcast.31, bf16[1,1,256,1536]{3,2,1,0:T(8,128)(2,1)} %bitcast.15, bf16[1,1,256,1536]{3,2,1,0:T(8,128)(2,1)S(1)} %bitcast.34), kind=kLoop, calls=%fused_computation.1 | loop fusion | flops 5505024 | bytes 6291456 | tf_op jit(solution)/shard_map/convert_element_type | solution.py:794
  (69 shorter events, 25.2 us)
Async XLA Ops:
  3.0 17.3 %collective-permute-start.2 = (bf16[128,2176]{1,0:T(8,128)(2,1)}, bf16[128,2176]{1,0:T(8,128)(2,1)S(1)}, u32[]{:S(2)}, u32[]{:S(2)}) collective-permute-start(bf16[128,2176]{1,0:T(8,128)(2,1)} %get-tuple-element.93.refs_0_), channel_id=1, source_target_pairs={{0,8},{1,9},{2,10},{3,11},{4,12},{5,13},{6,14},{7,15},{8,0},{9,1},... | collective-permute-start | bytes 1671176 | tf_op jit(solution)/shard_map/ppermute | solution.py:62
  6.1 25.1 %collective-permute-start.1 = (bf16[128,2176]{1,0:T(8,128)(2,1)}, bf16[128,2176]{1,0:T(8,128)(2,1)S(1)}, u32[]{:S(2)}, u32[]{:S(2)}) collective-permute-start(bf16[128,2176]{1,0:T(8,128)(2,1)} %get-tuple-element.93.refs_0_), channel_id=1, source_target_pairs={{0,12},{1,13},{2,14},{3,15},{4,0},{5,1},{6,2},{7,3},{8,4},{9,5},{1... | collective-permute-start | bytes 1671176 | tf_op jit(solution)/shard_map/ppermute | solution.py:62
  7.3 24.0 %collective-permute-start = (bf16[128,2176]{1,0:T(8,128)(2,1)}, bf16[128,2176]{1,0:T(8,128)(2,1)S(1)}, u32[]{:S(2)}, u32[]{:S(2)}) collective-permute-start(bf16[128,2176]{1,0:T(8,128)(2,1)} %get-tuple-element.93.refs_0_), channel_id=1, source_target_pairs={{0,4},{1,5},{2,6},{3,7},{4,8},{5,9},{6,10},{7,11},{8,12},{9,13},{1... | collective-permute-start | bytes 1671176 | tf_op jit(solution)/shard_map/ppermute | solution.py:62
  8.1 32.0 %collective-permute-start.5 = (bf16[128,2176]{1,0:T(8,128)(2,1)}, bf16[128,2176]{1,0:T(8,128)(2,1)S(1)}, u32[]{:S(2)}, u32[]{:S(2)}) collective-permute-start(bf16[128,2176]{1,0:T(8,128)(2,1)} %get-tuple-element.86.refs_0_), channel_id=1, source_target_pairs={{0,2},{1,3},{2,0},{3,1},{4,6},{5,7},{6,4},{7,5},{8,10},{9,11},{10,... | collective-permute-start | bytes 1671176 | tf_op jit(solution)/shard_map/ppermute | solution.py:62
  12.0 28.1 %collective-permute-start.4 = (bf16[128,2176]{1,0:T(8,128)(2,1)}, bf16[128,2176]{1,0:T(8,128)(2,1)S(1)}, u32[]{:S(2)}, u32[]{:S(2)}) collective-permute-start(bf16[128,2176]{1,0:T(8,128)(2,1)} %get-tuple-element.86.refs_0_), channel_id=1, source_target_pairs={{0,3},{1,0},{2,1},{3,2},{4,7},{5,4},{6,5},{7,6},{8,11},{9,8},{10,9... | collective-permute-start | bytes 1671176 | tf_op jit(solution)/shard_map/ppermute | solution.py:62
  20.3 10.9 %copy-start.13 = (bf16[128,2176]{1,0:T(8,128)(2,1)}, bf16[128,2176]{1,0:T(8,128)(2,1)S(1)}, u32[]{:S(2)}) copy-start(bf16[128,2176]{1,0:T(8,128)(2,1)S(1)} %collective-permute-done.2.refs_3_) | copy-start | bytes 1671172
  20.3 19.9 %collective-permute-start.3 = (bf16[128,2176]{1,0:T(8,128)(2,1)}, bf16[128,2176]{1,0:T(8,128)(2,1)}, u32[]{:S(2)}, u32[]{:S(2)}) collective-permute-start(bf16[128,2176]{1,0:T(8,128)(2,1)} %get-tuple-element.86.refs_0_), channel_id=1, source_target_pairs={{0,1},{1,2},{2,3},{3,0},{4,5},{5,6},{6,7},{7,4},{8,9},{9,10},{10,1... | collective-permute-start | bytes 1671176 | tf_op jit(solution)/shard_map/ppermute | solution.py:62
  36.0 30.1 %collective-permute-start.9 = (bf16[288,2048]{1,0:T(8,128)(2,1)}, bf16[288,2048]{1,0:T(8,128)(2,1)S(1)}, u32[]{:S(2)}, u32[]{:S(2)}) collective-permute-start(bf16[288,2048]{1,0:T(8,128)(2,1)} %get-tuple-element.95), channel_id=1, source_target_pairs={{0,1},{1,2},{2,3},{3,0},{4,5},{5,6},{6,7},{7,4},{8,9},{9,10},{10,1... | collective-permute-start | bytes 3538952 | tf_op jit(solution)/shard_map/ppermute | solution.py:62
  37.9 28.2 %collective-permute-start.10 = (bf16[288,2048]{1,0:T(8,128)(2,1)}, bf16[288,2048]{1,0:T(8,128)(2,1)S(1)}, u32[]{:S(2)}, u32[]{:S(2)}) collective-permute-start(bf16[288,2048]{1,0:T(8,128)(2,1)} %get-tuple-element.96), channel_id=1, source_target_pairs={{0,3},{1,0},{2,1},{3,2},{4,7},{5,4},{6,5},{7,6},{8,11},{9,8},{10,9... | collective-permute-start | bytes 3538952 | tf_op jit(solution)/shard_map/ppermute | solution.py:62
  45.3 28.8 %collective-permute-start.6 = (bf16[288,2048]{1,0:T(8,128)(2,1)}, bf16[288,2048]{1,0:T(8,128)(2,1)S(1)}, u32[]{:S(2)}, u32[]{:S(2)}) collective-permute-start(bf16[288,2048]{1,0:T(8,128)(2,1)} %get-tuple-element.89), channel_id=1, source_target_pairs={{0,4},{1,5},{2,6},{3,7},{4,8},{5,9},{6,10},{7,11},{8,12},{9,13},{1... | collective-permute-start | bytes 3538952 | tf_op jit(solution)/shard_map/ppermute | solution.py:62
  46.7 27.6 %collective-permute-start.7 = (bf16[288,2048]{1,0:T(8,128)(2,1)}, bf16[288,2048]{1,0:T(8,128)(2,1)S(1)}, u32[]{:S(2)}, u32[]{:S(2)}) collective-permute-start(bf16[288,2048]{1,0:T(8,128)(2,1)} %get-tuple-element.90), channel_id=1, source_target_pairs={{0,12},{1,13},{2,14},{3,15},{4,0},{5,1},{6,2},{7,3},{8,4},{9,5},{1... | collective-permute-start | bytes 3538952 | tf_op jit(solution)/shard_map/ppermute | solution.py:62
  66.1 7.6 %copy-start.3 = (bf16[288,2048]{1,0:T(8,128)(2,1)}, bf16[288,2048]{1,0:T(8,128)(2,1)S(1)}, u32[]{:S(2)}) copy-start(bf16[288,2048]{1,0:T(8,128)(2,1)S(1)} %collective-permute-done.9.refs_2_.refs_5_.refs_1_) | copy-start | bytes 3538948
  66.1 7.6 %copy-start.4 = (bf16[288,2048]{1,0:T(8,128)(2,1)}, bf16[288,2048]{1,0:T(8,128)(2,1)S(1)}, u32[]{:S(2)}) copy-start(bf16[288,2048]{1,0:T(8,128)(2,1)S(1)} %collective-permute-done.10.refs_3_.refs_6_.refs_2_) | copy-start | bytes 3538948
  66.1 28.9 %collective-permute-start.11 = (bf16[288,2048]{1,0:T(8,128)(2,1)}, bf16[288,2048]{1,0:T(8,128)(2,1)}, u32[]{:S(2)}, u32[]{:S(2)}) collective-permute-start(bf16[288,2048]{1,0:T(8,128)(2,1)} %get-tuple-element.101), channel_id=1, source_target_pairs={{0,2},{1,3},{2,0},{3,1},{4,6},{5,7},{6,4},{7,5},{8,10},{9,11},{10,... | collective-permute-start | bytes 3538952 | tf_op jit(solution)/shard_map/ppermute | solution.py:62
  74.1 3.1 %copy-start = (bf16[288,2048]{1,0:T(8,128)(2,1)}, bf16[288,2048]{1,0:T(8,128)(2,1)S(1)}, u32[]{:S(2)}) copy-start(bf16[288,2048]{1,0:T(8,128)(2,1)S(1)} %collective-permute-done.6.refs_4_.refs_2_) | copy-start | bytes 3538948
  74.4 2.8 %copy-start.1 = (bf16[288,2048]{1,0:T(8,128)(2,1)}, bf16[288,2048]{1,0:T(8,128)(2,1)S(1)}, u32[]{:S(2)}) copy-start(bf16[288,2048]{1,0:T(8,128)(2,1)S(1)} %collective-permute-done.7.refs_5_.refs_3_) | copy-start | bytes 3538948
  74.4 29.7 %collective-permute-start.8 = (bf16[288,2048]{1,0:T(8,128)(2,1)}, bf16[288,2048]{1,0:T(8,128)(2,1)S(1)}, u32[]{:S(2)}, u32[]{:S(2)}) collective-permute-start(bf16[288,2048]{1,0:T(8,128)(2,1)} %get-tuple-element.92), channel_id=1, source_target_pairs={{0,8},{1,9},{2,10},{3,11},{4,12},{5,13},{6,14},{7,15},{8,0},{9,1},... | collective-permute-start | bytes 3538952 | tf_op jit(solution)/shard_map/ppermute | solution.py:62
  117.3 21.6 %collective-permute-start.12 = (bf16[768,512]{1,0:T(8,128)(2,1)}, bf16[768,512]{1,0:T(8,128)(2,1)S(1)}, u32[]{:S(2)}, u32[]{:S(2)}) collective-permute-start(bf16[768,512]{1,0:T(8,128)(2,1)} %get-tuple-element.138), channel_id=1, source_target_pairs={{0,16},{16,32},{32,48},{48,0},{1,17},{17,33},{33,49},{49,1},{2,18}... | collective-permute-start | bytes 2359304 | tf_op jit(solution)/shard_map/ppermute | solution.py:54
  119.0 20.0 %collective-permute-start.13 = (bf16[768,512]{1,0:T(8,128)(2,1)}, bf16[768,512]{1,0:T(8,128)(2,1)S(1)}, u32[]{:S(2)}, u32[]{:S(2)}) collective-permute-start(bf16[768,512]{1,0:T(8,128)(2,1)} %get-tuple-element.139), channel_id=1, source_target_pairs={{0,48},{16,0},{32,16},{48,32},{1,49},{17,1},{33,17},{49,33},{2,50}... | collective-permute-start | bytes 2359304 | tf_op jit(solution)/shard_map/ppermute | solution.py:54
  120.6 67.1 %all-to-all-start = ((bf16[16,72,2048]{2,1,0:T(8,128)(2,1)}), bf16[16,72,2048]{2,1,0:T(8,128)(2,1)}, u32[]{:S(2)}, u32[]{:S(2)}) async-start(bf16[16,72,2048]{2,1,0:T(8,128)(2,1)} %get-tuple-element.123), calls=%async_computation | async-start | bytes 9437184 | tf_op jit(solution)/shard_map/all_to_all | solution.py:832
  139.0 9.5 %copy-start.9 = (bf16[768,512]{1,0:T(8,128)(2,1)}, bf16[768,512]{1,0:T(8,128)(2,1)S(1)}, u32[]{:S(2)}) copy-start(bf16[768,512]{1,0:T(8,128)(2,1)S(1)} %collective-permute-done.12) | copy-start | bytes 2359300
  139.0 9.4 %copy-start.11 = (bf16[768,512]{1,0:T(8,128)(2,1)}, bf16[768,512]{1,0:T(8,128)(2,1)S(1)}, u32[]{:S(2)}) copy-start(bf16[768,512]{1,0:T(8,128)(2,1)S(1)} %collective-permute-done.13) | copy-start | bytes 2359300
  139.0 38.9 %collective-permute-start.14 = (bf16[512,1536]{1,0:T(8,128)(2,1)}, bf16[512,1536]{1,0:T(8,128)(2,1)}, u32[]{:S(2)}, u32[]{:S(2)}) collective-permute-start(bf16[512,1536]{1,0:T(8,128)(2,1)} %get-tuple-element.140), channel_id=1, source_target_pairs={{0,16},{16,32},{32,48},{48,0},{1,17},{17,33},{33,49},{49,1},{2,18}... | collective-permute-start | bytes 4718600 | tf_op jit(solution)/shard_map/ppermute | solution.py:54
  139.5 38.5 %collective-permute-start.15 = (bf16[512,1536]{1,0:T(8,128)(2,1)}, bf16[512,1536]{1,0:T(8,128)(2,1)}, u32[]{:S(2)}, u32[]{:S(2)}) collective-permute-start(bf16[512,1536]{1,0:T(8,128)(2,1)} %get-tuple-element.141), channel_id=1, source_target_pairs={{0,48},{16,0},{32,16},{48,32},{1,49},{17,1},{33,17},{49,33},{2,50}... | collective-permute-start | bytes 4718600 | tf_op jit(solution)/shard_map/ppermute | solution.py:54
  148.4 3.9 %copy-start.8 = (bf16[768,512]{1,0:T(8,128)(2,1)S(1)}, bf16[768,512]{1,0:T(8,128)(2,1)}, u32[]{:S(2)}) copy-start(bf16[768,512]{1,0:T(8,128)(2,1)} %get-tuple-element.160) | copy-start | bytes 2359300
  152.3 25.6 %copy-start.7 = (bf16[512,1536]{1,0:T(8,128)(2,1)S(1)}, bf16[512,1536]{1,0:T(8,128)(2,1)}, u32[]{:S(2)}) copy-start(bf16[512,1536]{1,0:T(8,128)(2,1)} %get-tuple-element.157) | copy-start | bytes 4718596
  154.5 41.0 %collective-permute-start.19 = (bf16[384,512]{1,0:T(8,128)(2,1)}, bf16[384,512]{1,0:T(8,128)(2,1)}, u32[]{:S(2)}, u32[]{:S(2)}) collective-permute-start(bf16[384,512]{1,0:T(8,128)(2,1)} %get-tuple-element.167), channel_id=1, source_target_pairs={{0,16},{16,32},{32,48},{48,0},{1,17},{17,33},{33,49},{49,1},{2,18}... | collective-permute-start | bytes 1179656 | tf_op jit(solution)/shard_map/ppermute | solution.py:54
  154.5 41.0 %collective-permute-start.20 = (bf16[384,512]{1,0:T(8,128)(2,1)S(1)}, bf16[384,512]{1,0:T(8,128)(2,1)}, u32[]{:S(2)}, u32[]{:S(2)}) collective-permute-start(bf16[384,512]{1,0:T(8,128)(2,1)S(1)} %get-tuple-element.168), channel_id=1, source_target_pairs={{0,48},{16,0},{32,16},{48,32},{1,49},{17,1},{33,17},{49,33},{2,50}... | collective-permute-start | bytes 1179656 | tf_op jit(solution)/shard_map/ppermute | solution.py:54
  179.7 20.1 %collective-permute-start.17 = (bf16[256,1536]{1,0:T(8,128)(2,1)S(1)}, bf16[256,1536]{1,0:T(8,128)(2,1)S(1)}, u32[]{:S(2)}, u32[]{:S(2)}) collective-permute-start(bf16[256,1536]{1,0:T(8,128)(2,1)S(1)} %get-tuple-element.163), channel_id=1, source_target_pairs={{0,16},{16,32},{32,48},{48,0},{1,17},{17,33},{33,49},{49,1},{2,18}... | collective-permute-start | bytes 2359304 | tf_op jit(solution)/shard_map/ppermute | solution.py:54
  180.5 19.2 %collective-permute-start.18 = (bf16[256,1536]{1,0:T(8,128)(2,1)S(1)}, bf16[256,1536]{1,0:T(8,128)(2,1)}, u32[]{:S(2)}, u32[]{:S(2)}) collective-permute-start(bf16[256,1536]{1,0:T(8,128)(2,1)S(1)} %get-tuple-element.164), channel_id=1, source_target_pairs={{0,48},{16,0},{32,16},{48,32},{1,49},{17,1},{33,17},{49,33},{2,50}... | collective-permute-start | bytes 2359304 | tf_op jit(solution)/shard_map/ppermute | solution.py:54
  187.8 5.3 %copy-start.6 = (f32[512,1536]{1,0:T(8,128)S(1)}, f32[512,1536]{1,0:T(8,128)}, u32[]{:S(2)}) copy-start(f32[512,1536]{1,0:T(8,128)} %gate_up_own.1) | copy-start | bytes 9437188
  192.9 9.7 %collective-permute-start.16 = (bf16[128,2048]{1,0:T(8,128)(2,1)}, bf16[128,2048]{1,0:T(8,128)(2,1)S(1)}, u32[]{:S(2)}, u32[]{:S(2)}) collective-permute-start(bf16[128,2048]{1,0:T(8,128)(2,1)} %home.1), channel_id=1, source_target_pairs={{0,64},{64,0},{1,65},{65,1},{2,66},{66,2},{3,67},{67,3},{4,68},{68... | collective-permute-start | bytes 1572872 | tf_op jit(solution)/shard_map/ppermute | solution.py:54
  (8 other events, 11.2 us)
